TPU v7x, 128 devices: a whole 4x4x4 slice. The times are simulated.
128 devices in a mesh: ctx: 16 (over x, z), fsdp: 8 (over y, core).
Axes of the slice: x: 4, y: 4, z: 4, core: 2. Of those that a mesh axis runs over, the one named last changes fastest.
Arguments:
- tokens: bfloat16 [8, 4096, 1024], P('fsdp', 'ctx'), may hold values from -6 to 6
- cotangent: bfloat16 [8, 4096, 1024], P('fsdp', 'ctx'), may hold values from -6 to 6
- lengths: int32 [8, 4], P('fsdp'), may hold values from 1 to 2048, as said below
- input_gain: bfloat16 [1024], P('fsdp'), may hold values from 0.5 to 1.5
- query_weight: bfloat16 [1024, 512], P('fsdp'), may hold values from -0.1875 to 0.1875
- key_weight: bfloat16 [1024, 128], P('fsdp'), may hold values from -0.1875 to 0.1875
- value_weight: bfloat16 [1024, 128], P('fsdp'), may hold values from -0.1875 to 0.1875
- attention_out: bfloat16 [512, 1024], P('fsdp'), may hold values from -1 to 1
- mixer_in: bfloat16 [1024, 3072], P('fsdp'), may hold values from -0.1875 to 0.1875
- state_in: bfloat16 [1024, 256], P('fsdp'), may hold values from -0.046875 to 0.046875
- step_in: bfloat16 [1024, 24], P('fsdp'), may hold values from -0.1875 to 0.1875
- conv_weight: bfloat16 [4, 1792], P(None, 'fsdp'), may hold values from -3 to 3
- conv_bias: bfloat16 [1792], P('fsdp'), may hold values from -2 to 2
- step_bias: bfloat16 [24], P('fsdp'), may hold values from -3 to -0.5
- decay_log: bfloat16 [24], P('fsdp'), may hold values from -4 to -0.5
- skip_gain: bfloat16 [24], P('fsdp'), may hold values from 0.5 to 1.5
- mixer_out: bfloat16 [1536, 1024], P('fsdp'), may hold values from -0.0390625 to 0.0390625
- feed_gain: bfloat16 [1024], P('fsdp'), may hold values from 0.5 to 1.5
- gate_weight: bfloat16 [1024, 2048], P('fsdp'), may hold values from -0.1875 to 0.1875
- up_weight: bfloat16 [1024, 2048], P('fsdp'), may hold values from -0.1875 to 0.1875
- down_weight: bfloat16 [2048, 1024], P('fsdp'), may hold values from -0.125 to 0.125
Outputs:
- output: bfloat16 [8, 4096, 1024], P('fsdp', 'ctx')
- input_grad: float32 [8, 4096, 1024], P('fsdp', 'ctx')
- input_gain_gradient: float32 [1024], P('fsdp')
- query_weight_gradient: float32 [1024, 512], P('fsdp')
- key_weight_gradient: float32 [1024, 128], P('fsdp')
- value_weight_gradient: float32 [1024, 128], P('fsdp')
- attention_out_gradient: float32 [512, 1024], P('fsdp')
- mixer_in_gradient: float32 [1024, 3072], P('fsdp')
- state_in_gradient: float32 [1024, 256], P('fsdp')
- step_in_gradient: float32 [1024, 24], P('fsdp')
- conv_weight_gradient: float32 [4, 1792], P(None, 'fsdp')
- conv_bias_gradient: float32 [1792], P('fsdp')
- step_bias_gradient: float32 [24], P('fsdp')
- decay_log_gradient: float32 [24], P('fsdp')
- skip_gain_gradient: float32 [24], P('fsdp')
- mixer_out_gradient: float32 [1536, 1024], P('fsdp')
- feed_gain_gradient: float32 [1024], P('fsdp')
- gate_weight_gradient: float32 [1024, 2048], P('fsdp')
- up_weight_gradient: float32 [1024, 2048], P('fsdp')
- down_weight_gradient: float32 [2048, 1024], P('fsdp')
Inputs may be any that keep to these rules, and one draw needn't show every extreme that they name: In each sequence one document has exactly 2048 positions and is either the first or the last; the lengths of a sequence sum to 4096.
All inputs are finite; a program needn't handle non-finite values.
Results may differ from a plain program's by a relative error of at most 0.019.
The roundings to bfloat16 on the way count: a program that leaves them out, or rounds other values in their place, can miss the bound.
Values may be sent and summed in bfloat16 or wider, within the bound.
No kernel may reach another device: no remote copies, remote signals or barrier semaphores. Data moves between devices by JAX's collectives and lax.ppermute only.
A program may use at most 256 MiB of HBM per device.

v0:
```python
import jax
import jax.numpy as jnp
from jax import lax
from jax.sharding import PartitionSpec as P

HEADS = 8
KV_HEADS = 2
HEAD_DIM = 64
MIX_HEADS = 24
MIX_DIM = 64
STATE = 128
CONV = 4
QW = 512
KW = 128
MIX = 1536


EPSILON = 1e-05
ROPE_BASE = 100000000000.0
HIGHEST = lax.Precision.HIGHEST
NEG_LARGE = -1e30


def extended_2(x, sides, width):
    for axis, dim in sides:
        count, length = (lax.axis_size(axis), x.shape[dim])
        up = [(i, (i + 1) % count) for i in range(count - 1)]
        down = [(j, i) for i, j in up]
        last = lax.slice_in_dim(x, length - width, length, axis=dim)
        leading = lax.slice_in_dim(x, 0, width, axis=dim)
        before = lax.ppermute(last, axis, up)
        after = lax.ppermute(leading, axis, down)
        x = jnp.concatenate([before, x, after], axis=dim)
    return x


def carried_in(part, axis, combine, identity, reverse):
    count = lax.axis_size(axis)
    place = lax.axis_index(axis)
    ahead = count - 1 - place if reverse else place
    gathered = jax.tree.map(lambda a: lax.all_gather(a, axis), part)
    state = jax.tree.map(lambda a, e: jnp.zeros_like(a) + jnp.asarray(e, a.dtype), part, identity)

    def one(hop, state):
        source = count - 1 - hop if reverse else hop
        return combine(
            state, jax.tree.map(lambda a: lax.dynamic_index_in_dim(a, source, 0, False), gathered)
        )

    return lax.fori_loop(0, ahead, one, state)


def round_low(values):
    return lax.optimization_barrier(values.astype(jnp.bfloat16)).astype(jnp.float32)


def product(left, right):
    return jnp.dot(left, right, preferred_element_type=jnp.float32)


def left_product(left, right):
    return lax.dot_general(
        left, right, (((0,), (0,)), ((), ())), preferred_element_type=jnp.float32
    )


def right_product(left, right):
    return lax.dot_general(
        left, right, (((1,), (1,)), ((), ())), preferred_element_type=jnp.float32
    )


def rms_scale(values, gain_vector):
    return (
        values
        * lax.rsqrt(jnp.mean(values * values, axis=-1, keepdims=True) + EPSILON)
        * gain_vector
    )


def rope_tables(places):
    half_dim = HEAD_DIM // 2
    inverse = ROPE_BASE ** (-jnp.arange(half_dim, dtype=jnp.float32) / half_dim)
    angles = places.astype(jnp.float32)[:, None] * inverse[None, :]
    return (jnp.cos(angles), jnp.sin(angles))


def rotate(values, cosine, sine_part, head_count):
    token_count = values.shape[0]
    half_dim = HEAD_DIM // 2
    shaped = values.reshape(token_count, head_count, HEAD_DIM)
    lower_half = shaped[:, :, :half_dim]
    upper_half = shaped[:, :, half_dim:]
    cos_rows = cosine[:, None, :]
    sin_rows = sine_part[:, None, :]
    turned = jnp.concatenate(
        [
            lower_half * cos_rows - upper_half * sin_rows,
            upper_half * cos_rows + lower_half * sin_rows,
        ],
        axis=-1,
    )
    return turned.reshape(token_count, head_count * HEAD_DIM)


def unrotate(values, cosine, sine_part, head_count):
    token_count = values.shape[0]
    half_dim = HEAD_DIM // 2
    shaped = values.reshape(token_count, head_count, HEAD_DIM)
    lower_half = shaped[:, :, :half_dim]
    upper_half = shaped[:, :, half_dim:]
    cos_rows = cosine[:, None, :]
    sin_rows = sine_part[:, None, :]
    turned = jnp.concatenate(
        [
            lower_half * cos_rows + upper_half * sin_rows,
            upper_half * cos_rows - lower_half * sin_rows,
        ],
        axis=-1,
    )
    return turned.reshape(token_count, head_count * HEAD_DIM)


def document_ids(bounds, places):
    found_ids = jnp.sum((places[:, None] >= bounds[None, :-1]).astype(jnp.int32), axis=1)
    return jnp.where(places >= 0, found_ids, -1)


def conv_silu(extended, extended_doc, own_doc, taps, shift_bias):
    token_count = own_doc.shape[0]
    total_sum = jnp.zeros((token_count, extended.shape[1]), jnp.float32) + shift_bias[None, :]
    for offset in range(CONV):
        window = extended[offset : offset + token_count]
        same_doc = (extended_doc[offset : offset + token_count] == own_doc)[:, None]
        total_sum = total_sum + taps[offset][None, :] * jnp.where(same_doc, window, 0.0)
    return jax.nn.silu(total_sum)


def step_terms(step_raw, step_shift, decay_rate):
    step_size = jax.nn.softplus(step_raw + step_shift[None, :])
    cumulative = jnp.cumsum(-step_size * jnp.exp(decay_rate)[None, :], axis=0)
    return (step_size, cumulative)


def block_map(mix_values, write_keys, step_raw, step_shift, decay_rate, doc_ids, doc_before):
    step_size, cumulative = step_terms(step_raw, step_shift, decay_rate)
    final_sum = cumulative[-1]
    weight_in = (
        jnp.where((doc_ids == doc_ids[-1])[:, None], jnp.exp(final_sum[None, :] - cumulative), 0.0)
        * step_size
    )
    block_state = jnp.einsum("sh,shp,sn->hpn", weight_in, mix_values, write_keys, precision=HIGHEST)
    block_decay = jnp.where(doc_ids[-1] == doc_before, jnp.exp(final_sum), 0.0)
    return (block_decay, block_state)


def block_out(
    mix_values,
    write_keys,
    read_keys,
    step_raw,
    step_shift,
    decay_rate,
    skip_scale,
    doc_ids,
    doc_before,
    entry_state,
):
    step_size, cumulative = step_terms(step_raw, step_shift, decay_rate)
    token_count = doc_ids.shape[0]
    places = jnp.arange(token_count)
    allowed = (places[None, :] <= places[:, None]) & (doc_ids[None, :] == doc_ids[:, None])
    cum_heads = cumulative.T
    spread = cum_heads[:, :, None] - cum_heads[:, None, :]
    decays = jnp.where(allowed[None], jnp.exp(jnp.where(allowed[None], spread, 0.0)), 0.0)
    inner_sum = jnp.dot(read_keys, write_keys.T, precision=HIGHEST)
    mixing = decays * inner_sum[None]
    driven = step_size[:, :, None] * mix_values
    result = jnp.einsum("hts,shp->thp", mixing, driven, precision=HIGHEST)
    carried = jnp.where((doc_ids == doc_before)[:, None], jnp.exp(cumulative), 0.0)
    result = result + carried[:, :, None] * jnp.einsum(
        "hpn,tn->thp", entry_state, read_keys, precision=HIGHEST
    )
    return result + skip_scale[None, :, None] * mix_values


def compose(earlier, later):
    return (earlier[0] * later[0], later[0][:, None, None] * earlier[1] + later[1])


def compose_pair(earlier, later):
    return (compose(later[0], earlier[0]), compose(earlier[1], later[1]))


def apply_map(mapping, state_now):
    return mapping[0][:, None, None] * state_now + mapping[1]


def local(
    tokens,
    cotangent,
    lengths,
    input_gain,
    query_weight,
    key_weight,
    value_weight,
    attention_out,
    mixer_in,
    state_in,
    step_in,
    conv_weight,
    conv_bias,
    step_bias,
    decay_log,
    skip_gain,
    mixer_out,
    feed_gain,
    gate_weight,
    up_weight,
    down_weight,
):
    gathered = (
        lax.all_gather(input_gain, "fsdp", axis=0, tiled=True),
        lax.all_gather(query_weight, "fsdp", axis=0, tiled=True),
        lax.all_gather(key_weight, "fsdp", axis=0, tiled=True),
        lax.all_gather(value_weight, "fsdp", axis=0, tiled=True),
        lax.all_gather(attention_out, "fsdp", axis=0, tiled=True),
        lax.all_gather(mixer_in, "fsdp", axis=0, tiled=True),
        lax.all_gather(state_in, "fsdp", axis=0, tiled=True),
        lax.all_gather(step_in, "fsdp", axis=0, tiled=True),
        lax.all_gather(conv_weight, "fsdp", axis=1, tiled=True),
        lax.all_gather(conv_bias, "fsdp", axis=0, tiled=True),
        lax.all_gather(step_bias, "fsdp", axis=0, tiled=True),
        lax.all_gather(decay_log, "fsdp", axis=0, tiled=True),
        lax.all_gather(skip_gain, "fsdp", axis=0, tiled=True),
        lax.all_gather(mixer_out, "fsdp", axis=0, tiled=True),
        lax.all_gather(feed_gain, "fsdp", axis=0, tiled=True),
        lax.all_gather(gate_weight, "fsdp", axis=0, tiled=True),
        lax.all_gather(up_weight, "fsdp", axis=0, tiled=True),
        lax.all_gather(down_weight, "fsdp", axis=0, tiled=True),
    )
    (
        gain_whole,
        query_proj,
        key_proj,
        value_proj,
        attn_proj,
        mix_proj,
        state_proj,
        step_proj,
        conv_taps,
        conv_shift,
        step_shift,
        decay_rate,
        skip_scale,
        mix_out_proj,
        feed_whole,
        gate_proj,
        up_proj,
        down_proj,
    ) = gathered
    row_count = tokens.shape[1]
    half_rows = row_count // 2
    ctx_size = lax.axis_size("ctx")
    ctx_index = lax.axis_index("ctx")
    first_start = ctx_index * half_rows
    second_start = (2 * ctx_size - 1 - ctx_index) * half_rows
    offsets = jnp.arange(half_rows, dtype=jnp.int32)
    places = jnp.concatenate([first_start + offsets, second_start + offsets])
    bounds = jnp.cumsum(lengths[0])
    own_docs = document_ids(bounds, places)
    holders = jnp.arange(ctx_size, dtype=jnp.int32)[:, None]
    key_places = jnp.concatenate(
        [
            holders * half_rows + offsets[None, :],
            (2 * ctx_size - 1 - holders) * half_rows + offsets[None, :],
        ],
        axis=1,
    ).reshape(-1)
    key_docs = document_ids(bounds, key_places)
    cosine, sine_part = rope_tables(places)
    score_scale = HEAD_DIM ** (-0.5)
    group_size = HEADS // KV_HEADS
    pair_count = HEADS // 2
    pair_rows = 2 * row_count
    edge_width = CONV - 1
    x_rows = tokens[0].astype(jnp.float32)
    gain_in32 = gain_whole.astype(jnp.float32)
    normed = rms_scale(x_rows, gain_in32).astype(jnp.bfloat16)
    query_pre = product(normed, query_proj)
    key_pre = product(normed, key_proj)
    value_pre = product(normed, value_proj)
    queries = rotate(query_pre, cosine, sine_part, HEADS).astype(jnp.bfloat16)
    keys_rot = rotate(key_pre, cosine, sine_part, KV_HEADS).astype(jnp.bfloat16)
    values_low = value_pre.astype(jnp.bfloat16)
    keys_all, values_all = (
        lax.all_gather(keys_rot, "ctx", axis=0, tiled=True),
        lax.all_gather(values_low, "ctx", axis=0, tiled=True),
    )
    query_pairs = (
        queries.reshape(row_count, HEADS, HEAD_DIM)
        .transpose(1, 0, 2)
        .reshape(pair_count, pair_rows, HEAD_DIM)
    )
    key_heads = keys_all.reshape(-1, KV_HEADS, HEAD_DIM).transpose(1, 0, 2)
    value_heads = values_all.reshape(-1, KV_HEADS, HEAD_DIM).transpose(1, 0, 2)
    allowed = (key_places[None, :] <= places[:, None]) & (key_docs[None, :] == own_docs[:, None])
    allowed = jnp.concatenate([allowed, allowed], axis=0)

    def pair_scores(pair_index):
        query_block = query_pairs[pair_index]
        head_index = 2 * pair_index // group_size
        scores = right_product(query_block, key_heads[head_index]) * score_scale
        return (query_block, head_index, jnp.where(allowed, scores, NEG_LARGE))

    def attend(pair_index):
        _, head_index, scores = pair_scores(pair_index)
        row_peak = jnp.max(scores, axis=1, keepdims=True)
        shifted_exp = jnp.exp(scores - row_peak)
        row_total = jnp.sum(shifted_exp, axis=1, keepdims=True)
        weights = (shifted_exp / row_total).astype(jnp.bfloat16)
        return (
            product(weights, value_heads[head_index]),
            row_peak[:, 0] + jnp.log(row_total[:, 0]),
        )

    attended, log_totals = lax.map(attend, jnp.arange(pair_count))
    attended = (
        attended.reshape(HEADS, row_count, HEAD_DIM).transpose(1, 0, 2).reshape(row_count, QW)
    )
    attended_low = attended.astype(jnp.bfloat16)
    attn_branch = product(attended_low, attn_proj)
    mixed_in = product(normed, mix_proj).astype(jnp.bfloat16)
    state_part = product(normed, state_proj).astype(jnp.bfloat16)
    steps_raw = product(normed, step_proj)
    conv_in = jnp.concatenate([mixed_in[:, MIX:], state_part], axis=1)
    tails = jnp.stack(
        [conv_in[row_count - edge_width :], conv_in[half_rows - edge_width : half_rows]]
    )
    edges = extended_2(tails, (("ctx", 0),), 1)
    is_last = ctx_index == ctx_size - 1
    before_first = edges[0]
    before_second = jnp.where(is_last, tails[1], edges[3])
    taps32 = conv_taps.astype(jnp.float32)
    shift32 = conv_shift.astype(jnp.float32)
    step_shift32 = step_shift.astype(jnp.float32)
    decay32 = decay_rate.astype(jnp.float32)
    skip32 = skip_scale.astype(jnp.float32)
    edge_offsets = jnp.arange(-edge_width, half_rows, dtype=jnp.int32)
    first_ext_docs = document_ids(bounds, first_start + edge_offsets)
    second_ext_docs = document_ids(bounds, second_start + edge_offsets)
    first_docs = own_docs[:half_rows]
    second_docs = own_docs[half_rows:]
    first_before = document_ids(bounds, jnp.reshape(first_start - 1, (1,)))[0]
    second_before = document_ids(bounds, jnp.reshape(second_start - 1, (1,)))[0]
    first_ext = jnp.concatenate([before_first, conv_in[:half_rows]], axis=0).astype(jnp.float32)
    second_ext = jnp.concatenate([before_second, conv_in[half_rows:]], axis=0).astype(jnp.float32)
    conv_first = round_low(conv_silu(first_ext, first_ext_docs, first_docs, taps32, shift32))
    conv_second = round_low(conv_silu(second_ext, second_ext_docs, second_docs, taps32, shift32))
    values_first = conv_first[:, :MIX].reshape(half_rows, MIX_HEADS, MIX_DIM)
    write_first = conv_first[:, MIX : MIX + STATE]
    read_first = conv_first[:, MIX + STATE :]
    values_second = conv_second[:, :MIX].reshape(half_rows, MIX_HEADS, MIX_DIM)
    write_second = conv_second[:, MIX : MIX + STATE]
    read_second = conv_second[:, MIX + STATE :]
    raw_first = steps_raw[:half_rows]
    raw_second = steps_raw[half_rows:]
    decay_first, state_first = block_map(
        values_first, write_first, raw_first, step_shift32, decay32, first_docs, first_before
    )
    decay_second, state_second = block_map(
        values_second, write_second, raw_second, step_shift32, decay32, second_docs, second_before
    )
    identity = (
        jnp.ones((MIX_HEADS,), jnp.float32),
        jnp.zeros((MIX_HEADS, MIX_DIM, STATE), jnp.float32),
    )
    prefix = carried_in((decay_first, state_first), "ctx", compose, identity, False)
    entry_first = prefix[1]
    exit_first = apply_map((decay_first, state_first), entry_first)
    suffix = carried_in(
        ((decay_first, state_first), (decay_second, state_second)),
        "ctx",
        compose_pair,
        (identity, identity),
        True,
    )
    entry_second = apply_map(suffix[1], apply_map(suffix[0], exit_first))
    scan_first = block_out(
        values_first,
        write_first,
        read_first,
        raw_first,
        step_shift32,
        decay32,
        skip32,
        first_docs,
        first_before,
        entry_first,
    )
    scan_second = block_out(
        values_second,
        write_second,
        read_second,
        raw_second,
        step_shift32,
        decay32,
        skip32,
        second_docs,
        second_before,
        entry_second,
    )
    scanned = jnp.concatenate([scan_first, scan_second], axis=0).reshape(row_count, MIX)
    gate_z = mixed_in[:, :MIX].astype(jnp.float32)
    gated_low = (scanned * jax.nn.silu(gate_z)).astype(jnp.bfloat16)
    mix_branch = product(gated_low, mix_out_proj)
    middle = x_rows + attn_branch + mix_branch
    feed32 = feed_whole.astype(jnp.float32)
    normed_ff = rms_scale(middle, feed32).astype(jnp.bfloat16)
    gate_vals = product(normed_ff, gate_proj)
    up_vals = product(normed_ff, up_proj)
    activ = (jax.nn.silu(gate_vals) * up_vals).astype(jnp.bfloat16)
    output = (middle + product(activ, down_proj)).astype(jnp.bfloat16)
    grad_out = cotangent[0]
    d_activ = right_product(grad_out, down_proj)
    d_down = left_product(activ, grad_out)
    sig_gate = jax.nn.sigmoid(gate_vals)
    d_gate = (d_activ * up_vals * sig_gate * (1.0 + gate_vals * (1.0 - sig_gate))).astype(
        jnp.bfloat16
    )
    d_up = (d_activ * gate_vals * sig_gate).astype(jnp.bfloat16)
    d_gate_proj = left_product(normed_ff, d_gate)
    d_up_proj = left_product(normed_ff, d_up)
    d_normed_ff = right_product(d_gate, gate_proj) + right_product(d_up, up_proj)
    _, feed_pull = jax.vjp(rms_scale, middle, feed32)
    d_middle_norm, d_feed_gain = feed_pull(d_normed_ff)
    d_middle = grad_out.astype(jnp.float32) + d_middle_norm
    d_middle_low = d_middle.astype(jnp.bfloat16)
    d_mix_out_proj = left_product(gated_low, d_middle_low)
    d_gated = round_low(right_product(d_middle_low, mix_out_proj))
    sig_z = jax.nn.sigmoid(gate_z)
    d_scanned = d_gated * gate_z * sig_z
    d_gate_z = d_gated * scanned * sig_z * (1.0 + gate_z * (1.0 - sig_z))
    d_scan_first = d_scanned[:half_rows].reshape(half_rows, MIX_HEADS, MIX_DIM)
    d_scan_second = d_scanned[half_rows:].reshape(half_rows, MIX_HEADS, MIX_DIM)

    def out_pullback(
        mix_values, write_keys, read_keys, step_raw, doc_ids, doc_before, entry_state, upstream
    ):

        def local_out(values_in, write_in, read_in, raw_in, shift_in, rate_in, skip_in, entry_in):
            return block_out(
                values_in,
                write_in,
                read_in,
                raw_in,
                shift_in,
                rate_in,
                skip_in,
                doc_ids,
                doc_before,
                entry_in,
            )

        _, pullback = jax.vjp(
            local_out,
            mix_values,
            write_keys,
            read_keys,
            step_raw,
            step_shift32,
            decay32,
            skip32,
            entry_state,
        )
        return pullback(upstream)

    def map_pullback(
        mix_values, write_keys, step_raw, doc_ids, doc_before, entry_state, after_state
    ):

        def local_map(values_in, write_in, raw_in, shift_in, rate_in):
            return block_map(values_in, write_in, raw_in, shift_in, rate_in, doc_ids, doc_before)

        _, pullback = jax.vjp(local_map, mix_values, write_keys, step_raw, step_shift32, decay32)
        return pullback((jnp.sum(after_state * entry_state, axis=(1, 2)), after_state))

    out_first = out_pullback(
        values_first,
        write_first,
        read_first,
        raw_first,
        first_docs,
        first_before,
        entry_first,
        d_scan_first,
    )
    out_second = out_pullback(
        values_second,
        write_second,
        read_second,
        raw_second,
        second_docs,
        second_before,
        entry_second,
        d_scan_second,
    )
    adjoint_low = carried_in((decay_second, out_second[7]), "ctx", compose, identity, False)
    after_second = adjoint_low[1]
    before_second_adj = apply_map((decay_second, out_second[7]), after_second)
    adjoint_high = carried_in(
        ((decay_second, out_second[7]), (decay_first, out_first[7])),
        "ctx",
        compose_pair,
        (identity, identity),
        True,
    )
    after_first = apply_map(adjoint_high[1], apply_map(adjoint_high[0], before_second_adj))
    map_first = map_pullback(
        values_first, write_first, raw_first, first_docs, first_before, entry_first, after_first
    )
    map_second = map_pullback(
        values_second,
        write_second,
        raw_second,
        second_docs,
        second_before,
        entry_second,
        after_second,
    )
    d_conv_out_first = jnp.concatenate(
        [
            (out_first[0] + map_first[0]).reshape(half_rows, MIX),
            out_first[1] + map_first[1],
            out_first[2],
        ],
        axis=1,
    )
    d_conv_out_second = jnp.concatenate(
        [
            (out_second[0] + map_second[0]).reshape(half_rows, MIX),
            out_second[1] + map_second[1],
            out_second[2],
        ],
        axis=1,
    )
    d_raw = jnp.concatenate([out_first[3] + map_first[2], out_second[3] + map_second[2]], axis=0)
    d_step_shift = out_first[4] + out_second[4] + map_first[3] + map_second[3]
    d_decay = out_first[5] + out_second[5] + map_first[4] + map_second[4]
    d_skip = out_first[6] + out_second[6]

    def conv_pullback(extended, extended_doc, own_doc, upstream):

        def local_conv(ext_in, taps_in, shift_in):
            return conv_silu(ext_in, extended_doc, own_doc, taps_in, shift_in)

        _, pullback = jax.vjp(local_conv, extended, taps32, shift32)
        return pullback(upstream)

    d_ext_first, d_taps_first, d_shift_first = conv_pullback(
        first_ext, first_ext_docs, first_docs, d_conv_out_first
    )
    d_ext_second, d_taps_second, d_shift_second = conv_pullback(
        second_ext, second_ext_docs, second_docs, d_conv_out_second
    )
    edge_grads = extended_2(
        jnp.stack([d_ext_first[:edge_width], d_ext_second[:edge_width]]), (("ctx", 0),), 1
    )
    into_first_tail = edge_grads[3] + jnp.where(is_last, d_ext_second[:edge_width], 0.0)
    into_second_tail = edge_grads[0]
    d_conv_first = d_ext_first[edge_width:].at[half_rows - edge_width :].add(into_first_tail)
    d_conv_second = d_ext_second[edge_width:].at[half_rows - edge_width :].add(into_second_tail)
    d_conv_in = jnp.concatenate([d_conv_first, d_conv_second], axis=0)
    d_mixed = jnp.concatenate([d_gate_z, d_conv_in[:, :MIX]], axis=1).astype(jnp.bfloat16)
    d_state = d_conv_in[:, MIX:].astype(jnp.bfloat16)
    d_steps = d_raw.astype(jnp.bfloat16)
    d_mix_proj = left_product(normed, d_mixed)
    d_state_proj = left_product(normed, d_state)
    d_step_proj = left_product(normed, d_steps)
    d_normed = (
        right_product(d_mixed, mix_proj)
        + right_product(d_state, state_proj)
        + right_product(d_steps, step_proj)
    )
    d_attended = right_product(d_middle_low, attn_proj).astype(jnp.bfloat16)
    d_attn_proj = left_product(attended_low, d_middle_low)
    d_attended_pairs = (
        d_attended.reshape(row_count, HEADS, HEAD_DIM)
        .transpose(1, 0, 2)
        .reshape(pair_count, pair_rows, HEAD_DIM)
    )

    def attend_back(pair_index):
        query_block, head_index, scores = pair_scores(pair_index)
        weights = jnp.exp(scores - log_totals[pair_index][:, None])
        upstream = d_attended_pairs[pair_index]
        d_weights = right_product(upstream, value_heads[head_index])
        inner_sum = jnp.sum(weights * d_weights, axis=1, keepdims=True)
        d_scores = (weights * (d_weights - inner_sum)).astype(jnp.bfloat16)
        d_query = product(d_scores, key_heads[head_index]) * score_scale
        d_key = left_product(d_scores, query_block) * score_scale
        d_value = left_product(weights.astype(jnp.bfloat16), upstream)
        return (d_query, d_key, d_value)

    d_query_pairs, d_key_pairs, d_value_pairs = lax.map(attend_back, jnp.arange(pair_count))
    pairs_per_head = group_size // 2
    d_keys = (
        d_key_pairs.reshape(KV_HEADS, pairs_per_head, -1, HEAD_DIM)
        .sum(axis=1)
        .transpose(1, 0, 2)
        .reshape(-1, KW)
    )
    d_values = (
        d_value_pairs.reshape(KV_HEADS, pairs_per_head, -1, HEAD_DIM)
        .sum(axis=1)
        .transpose(1, 0, 2)
        .reshape(-1, KW)
    )
    d_keys_own, d_values_own = (
        lax.psum_scatter(d_keys, "ctx", scatter_dimension=0, tiled=True),
        lax.psum_scatter(d_values, "ctx", scatter_dimension=0, tiled=True),
    )
    d_queries = (
        d_query_pairs.reshape(HEADS, row_count, HEAD_DIM).transpose(1, 0, 2).reshape(row_count, QW)
    )
    d_query_pre = unrotate(d_queries, cosine, sine_part, HEADS).astype(jnp.bfloat16)
    d_key_pre = unrotate(d_keys_own, cosine, sine_part, KV_HEADS).astype(jnp.bfloat16)
    d_value_pre = d_values_own.astype(jnp.bfloat16)
    d_query_proj = left_product(normed, d_query_pre)
    d_key_proj = left_product(normed, d_key_pre)
    d_value_proj = left_product(normed, d_value_pre)
    d_normed = (
        d_normed
        + right_product(d_query_pre, query_proj)
        + right_product(d_key_pre, key_proj)
        + right_product(d_value_pre, value_proj)
    )
    _, input_pull = jax.vjp(rms_scale, x_rows, gain_in32)
    d_rows_norm, d_input_gain = input_pull(d_normed)
    input_grad = (d_middle + d_rows_norm)[None]
    gradients = (
        d_input_gain,
        d_query_proj,
        d_key_proj,
        d_value_proj,
        d_attn_proj,
        d_mix_proj,
        d_state_proj,
        d_step_proj,
        d_taps_first + d_taps_second,
        d_shift_first + d_shift_second,
        d_step_shift,
        d_decay,
        d_skip,
        d_mix_out_proj,
        d_feed_gain,
        d_gate_proj,
        d_up_proj,
        d_down,
    )
    shards_out = (
        lax.psum_scatter(gradients[0], "fsdp", scatter_dimension=0, tiled=True),
        lax.psum_scatter(gradients[1], "fsdp", scatter_dimension=0, tiled=True),
        lax.psum_scatter(gradients[2], "fsdp", scatter_dimension=0, tiled=True),
        lax.psum_scatter(gradients[3], "fsdp", scatter_dimension=0, tiled=True),
        lax.psum_scatter(gradients[4], "fsdp", scatter_dimension=0, tiled=True),
        lax.psum_scatter(gradients[5], "fsdp", scatter_dimension=0, tiled=True),
        lax.psum_scatter(gradients[6], "fsdp", scatter_dimension=0, tiled=True),
        lax.psum_scatter(gradients[7], "fsdp", scatter_dimension=0, tiled=True),
        lax.psum_scatter(gradients[8], "fsdp", scatter_dimension=1, tiled=True),
        lax.psum_scatter(gradients[9], "fsdp", scatter_dimension=0, tiled=True),
        lax.psum_scatter(gradients[10], "fsdp", scatter_dimension=0, tiled=True),
        lax.psum_scatter(gradients[11], "fsdp", scatter_dimension=0, tiled=True),
        lax.psum_scatter(gradients[12], "fsdp", scatter_dimension=0, tiled=True),
        lax.psum_scatter(gradients[13], "fsdp", scatter_dimension=0, tiled=True),
        lax.psum_scatter(gradients[14], "fsdp", scatter_dimension=0, tiled=True),
        lax.psum_scatter(gradients[15], "fsdp", scatter_dimension=0, tiled=True),
        lax.psum_scatter(gradients[16], "fsdp", scatter_dimension=0, tiled=True),
        lax.psum_scatter(gradients[17], "fsdp", scatter_dimension=0, tiled=True),
    )
    totals = lax.psum(
        (
            shards_out[0],
            shards_out[1],
            shards_out[2],
            shards_out[3],
            shards_out[4],
            shards_out[5],
            shards_out[6],
            shards_out[7],
            shards_out[8],
            shards_out[9],
            shards_out[10],
            shards_out[11],
            shards_out[12],
            shards_out[13],
            shards_out[14],
            shards_out[15],
            shards_out[16],
            shards_out[17],
        ),
        "ctx",
    )
    return (output[None], input_grad) + tuple(totals)


def solution(mesh):
    return jax.shard_map(
        local,
        mesh=mesh,
        in_specs=(
            P("fsdp", "ctx", None),
            P("fsdp", "ctx", None),
            P("fsdp", None),
            P("fsdp"),
            P("fsdp", None),
            P("fsdp", None),
            P("fsdp", None),
            P("fsdp", None),
            P("fsdp", None),
            P("fsdp", None),
            P("fsdp", None),
            P(None, "fsdp"),
            P("fsdp"),
            P("fsdp"),
            P("fsdp"),
            P("fsdp"),
            P("fsdp", None),
            P("fsdp"),
            P("fsdp", None),
            P("fsdp", None),
            P("fsdp", None),
        ),
        out_specs=(
            P("fsdp", "ctx", None),
            P("fsdp", "ctx", None),
            P("fsdp"),
            P("fsdp", None),
            P("fsdp", None),
            P("fsdp", None),
            P("fsdp", None),
            P("fsdp", None),
            P("fsdp", None),
            P("fsdp", None),
            P(None, "fsdp"),
            P("fsdp"),
            P("fsdp"),
            P("fsdp"),
            P("fsdp"),
            P("fsdp", None),
            P("fsdp"),
            P("fsdp", None),
            P("fsdp", None),
            P("fsdp", None),
        ),
        check_vma=False,
    )
```

profile of v0, /device:TPU:0, one launch (start us, length us, event | category | flops | bytes accessed | tf_op | source)
XLA Modules:
  0.0 1677.2 jit_solution(15659498903221386566)
XLA Ops:
  140.8 24.8 %all-gather.6 = f32[16,1,24]{2,1,0:T(1,128)S(1)} all-gather(f32[1,1,24]{2,1,0:T(1,128)S(1)} %get-tuple-element.1029), channel_id=1, replica_groups=mesh['ctx'=16,'fsdp'=8] {'ctx'}, dimensions={0}, use_global_device_ids=true | all-gather | bytes 1632 | tf_op jit(solution)/shard_map/all_gather | solution.py:41
  165.6 18.9 %all-gather.7 = f32[16,1,24]{2,1,0:T(1,128)S(1)} all-gather(f32[1,1,24]{2,1,0:T(1,128)S(1)} %get-tuple-element.1027), channel_id=1, replica_groups=mesh['ctx'=16,'fsdp'=8] {'ctx'}, dimensions={0}, use_global_device_ids=true | all-gather | bytes 1632 | tf_op jit(solution)/shard_map/all_gather | solution.py:41
  207.0 39.5 %while.92 = (s32[]{:T(128)}, bf16[4,512,64]{1,2,0:T(8,128)(2,1)S(1)}, f32[4,512]{1,0:T(4,128)S(1)}, s32[4]{0:T(128)S(1)}, bf16[4,512,64]{2,1,0:T(8,128)(2,1)S(1)...) while((s32[]{:T(128)}, ...), condition=%wide.region_7.8_spmd, body=%wide.region_4.7_spmd.sunk | while | flops 553647616 | bytes 33837484 | solution.py:327
  265.4 90.1 %all-gather.43.cloned.1.call-done = f32[384,64,128]{2,1,0:T(8,128)} async-done(((f32[24,64,128]{2,1,0:T(8,128)}), f32[384,64,128]{2,1,0:T(8,128)}) %all-gather.43.cloned.1.call-update) | async-done | bytes 12582928 | tf_op jit(solution)/shard_map/all_gather | solution.py:41
  357.4 49.6 %while.94 = (s32[]{:T(128)}, f32[24]{0:T(128)S(1)}, f32[24,64,128]{2,1,0:T(8,128)}, f32[24]{0:T(128)S(1)}, f32[24,64,128]{2,1,0:T(8,128)}, /*index=5*/s32[]{:T(1...) while((s32[]{:T(128)}, f32[24]{0:T(128)S(1)}, ...), condition=%wide.region_17.18_spmd, body=%wide.region_16.17_spmd.sunk | while | flops 786486 | bytes 4719655 | solution.py:50
  448.2 28.8 %all-gather.37.cloned.1.call-done = bf16[1024,2048]{1,0:T(8,128)(2,1)} async-done(((bf16[128,2048]{1,0:T(8,128)(2,1)}), bf16[1024,2048]{1,0:T(8,128)(2,1)}) %all-gather.37.cloned.1.call-update) | async-done | bytes 4194320 | tf_op jit(solution)/shard_map/all_gather | solution.py:239
  482.0 28.9 %all-gather.39.cloned.1.call-done = bf16[2048,1024]{1,0:T(8,128)(2,1)} async-done(((bf16[256,1024]{1,0:T(8,128)(2,1)}), bf16[2048,1024]{1,0:T(8,128)(2,1)}) %all-gather.39.cloned.1.call-update) | async-done | bytes 4194320 | tf_op jit(solution)/shard_map/all_gather | solution.py:240
  525.6 147.1 %while.97 = (s32[]{:T(128)}, f32[4,512,64]{1,0,2:T(4,128)}, f32[4,4096,64]{1,2,0:T(8,128)}, f32[4,4096,64]{1,2,0:T(8,128)}, s32[4]{0:T(128)S(1)}, /*index=5*/bf1...) while((s32[]{:T(128)}, f32[4,512,64]{1,0,2:T(4,128)}, ...), condition=%wide.region_46.48_spmd, body=%wide.region_44.47_spmd.sunk | while | flops 1361346048 | bytes 128068160 | solution.py:605
  697.8 53.6 %reduce-scatter.17.cloned.1.call-done = f32[256,128]{0,1:T(8,128)} async-done(((f32[4096,128]{0,1:T(8,128)}), f32[256,128]{0,1:T(8,128)}) %reduce-scatter.17.cloned.1.call-update) | async-done | bytes 131088 | tf_op jit(solution)/shard_map/reduce_scatter | solution.py:620
  753.7 75.1 %reduce-scatter.19.cloned.1.call-done = f32[256,128]{0,1:T(8,128)} async-done(((f32[4096,128]{0,1:T(8,128)}), f32[256,128]{0,1:T(8,128)}) %reduce-scatter.19.cloned.1.call-update) | async-done | bytes 131088 | tf_op jit(solution)/shard_map/reduce_scatter | solution.py:621
  878.2 41.9 %all-gather.45.cloned.1.call-done = f32[384,64,128]{2,1,0:T(8,128)} async-done(((f32[24,64,128]{2,1,0:T(8,128)}), f32[384,64,128]{2,1,0:T(8,128)}) %all-gather.45.cloned.1.call-update) | async-done | bytes 12582928 | tf_op jit(solution)/shard_map/all_gather | solution.py:41
  927.3 84.5 %all-gather.47.cloned.1.call-done = f32[384,64,128]{2,1,0:T(8,128)} async-done(((f32[24,64,128]{2,1,0:T(8,128)}), f32[384,64,128]{2,1,0:T(8,128)}) %all-gather.47.cloned.1.call-update) | async-done | bytes 12582928 | tf_op jit(solution)/shard_map/all_gather | solution.py:41
  1012.9 61.0 %while.95 = (s32[]{:T(128)}, f32[24]{0:T(128)S(1)}, f32[24,64,128]{2,1,0:T(8,128)S(1)}, f32[24]{0:T(128)S(1)}, f32[24,64,128]{2,1,0:T(8,128)}, /*index=5*/s32[]{...) while((s32[]{:T(128)}, f32[24]{0:T(128)S(1)}, ...), condition=%wide.region_23.25_spmd, body=%wide.region_22.24_spmd.sunk | while | flops 786486 | bytes 4719655 | solution.py:50
  1123.8 22.7 %reduce-scatter.25.cloned.1.call-done = f32[128,128]{1,0:T(8,128)} async-done(((f32[1024,128]{1,0:T(8,128)}), f32[128,128]{1,0:T(8,128)}) %reduce-scatter.25.cloned.1.call-update) | async-done | bytes 65552 | tf_op jit(solution)/shard_map/reduce_scatter | solution.py:665
  1146.5 43.6 %reduce-scatter.35.cloned.1.call-done = f32[192,1024]{1,0:T(8,128)} async-done(((f32[1536,1024]{1,0:T(8,128)}), f32[192,1024]{1,0:T(8,128)}) %reduce-scatter.35.cloned.1.call-update) | async-done | bytes 786448 | tf_op jit(solution)/shard_map/reduce_scatter | solution.py:675
  1190.1 54.6 %reduce-scatter.37.cloned.1.call-done = f32[128,2048]{1,0:T(8,128)} async-done(((f32[1024,2048]{1,0:T(8,128)}), f32[128,2048]{1,0:T(8,128)}) %reduce-scatter.37.cloned.1.call-update) | async-done | bytes 1048592 | tf_op jit(solution)/shard_map/reduce_scatter | solution.py:677
  1244.7 54.5 %reduce-scatter.39.cloned.1.call-done = f32[128,2048]{1,0:T(8,128)} async-done(((f32[1024,2048]{1,0:T(8,128)}), f32[128,2048]{1,0:T(8,128)}) %reduce-scatter.39.cloned.1.call-update) | async-done | bytes 1048592 | tf_op jit(solution)/shard_map/reduce_scatter | solution.py:678
  1299.2 54.5 %reduce-scatter.41.cloned.1.call-done = f32[256,1024]{1,0:T(8,128)} async-done(((f32[2048,1024]{1,0:T(8,128)}), f32[256,1024]{1,0:T(8,128)}) %reduce-scatter.41.cloned.1.call-update) | async-done | bytes 1048592 | tf_op jit(solution)/shard_map/reduce_scatter | solution.py:679
  1353.6 34.3 %reduce-scatter.31.cloned.1.call-done = f32[128,256]{1,0:T(8,128)} async-done(((f32[1024,256]{1,0:T(8,128)}), f32[128,256]{1,0:T(8,128)}) %reduce-scatter.31.cloned.1.call-update) | async-done | bytes 131088 | tf_op jit(solution)/shard_map/reduce_scatter | solution.py:668
  1388.0 73.6 %reduce-scatter.29.cloned.1.call-done = f32[128,3072]{1,0:T(8,128)} async-done(((f32[1024,3072]{1,0:T(8,128)}), f32[128,3072]{1,0:T(8,128)}) %reduce-scatter.29.cloned.1.call-update) | async-done | bytes 1572880 | tf_op jit(solution)/shard_map/reduce_scatter | solution.py:667
  1478.4 23.6 %all-reduce.30 = (f32[1024]{0:T(1024)S(1)}, f32[1792]{0:T(1024)S(1)}, f32[24]{0:T(128)S(1)}, f32[24]{0:T(128)S(1)}, f32[24]{0:T(128)S(1)}, /*index=5*/f32[1024]{0:T(1024)S(1)}) all-reduce(f32[1024]{0:T(1024)S(1)} %get-tuple-element.792, f32[1792]{0:T(1024)S(1)} %add.696, ...), channel_id=8, replica_groups=mesh['ctx'=16,'fsdp'=8] {'fsdp'}, use_global_device_ids=true, to_apply=%region_53.55.clone | all-reduce | flops 3912 | bytes 31296
  1506.2 21.5 %reduce-scatter.33.cloned.1.call-done = f32[128,24]{0,1:T(8,128)} async-done(((f32[1024,24]{0,1:T(8,128)}), f32[128,24]{0,1:T(8,128)}) %reduce-scatter.33.cloned.1.call-update) | async-done | bytes 12304 | tf_op jit(solution)/shard_map/reduce_scatter | solution.py:669
  1527.7 76.0 %all-reduce.28 = (f32[128]{0:T(128)}, f32[128,24]{0,1:T(8,128)}, f32[4,224]{1,0:T(4,128)}, f32[224]{0:T(256)}, f32[3]{0:T(128)}, /*index=5*/f32[3]{0:T(128)}, f32[3]{0:T(128)}, f32[128]{0:T(128)}) all-reduce(f32[128]{0:T(128)S(1)} %dynamic-slice.20, ...), channel_id=1, replica_groups=mesh['ctx'=16,'fsdp'=8] {'ctx'}, use_global_device_ids=true, to_apply=%region_54.56 | all-reduce | flops 4457 | bytes 35656 | tf_op jit(solution)/shard_map/psum | solution.py:681
  1603.7 52.7 %all-reduce.34.cloned.1.call-done = (f32[128,512]{1,0:T(8,128)}, f32[128,128]{1,0:T(8,128)}, f32[128,128]{1,0:T(8,128)}, f32[64,1024]{1,0:T(8,128)}, f32[128,307...) async-done(((f32[128,512]{1,0:T(8,128)}, f32[128,128]{1,0:T(8,128)}, ...) | async-done | bytes 6291472 | tf_op jit(solution)/shard_map/psum | solution.py:681
  (984 shorter events, 672.9 us)
Async XLA Ops:
  8.7 190.6 %all-gather.25.cloned.1.call-start = ((), (), s32[]{:S(2)}) async-start(), calls=%async_computation.15 | async-start | bytes 1114112 | tf_op jit(solution)/shard_map/all_gather | solution.py:297
  51.7 211.4 %all-gather.41.cloned.1.call-start = ((), (), s32[]{:S(2)}) async-start(), calls=%async_computation.36 | async-start | bytes 13369344 | tf_op jit(solution)/shard_map/all_gather | solution.py:41
  130.3 225.2 %all-gather.43.cloned.1.call-start = ((), (), s32[]{:S(2)}) async-start(), calls=%async_computation.37 | async-start | bytes 13369344 | tf_op jit(solution)/shard_map/all_gather | solution.py:41
  136.4 288.2 %all-gather.33.cloned.1.call-start = ((), (), s32[]{:S(2)}) async-start(), calls=%async_computation.19 | async-start | bytes 3538944 | tf_op jit(solution)/shard_map/all_gather | solution.py:236
  137.2 291.6 %all-gather.29.cloned.1.call-start = ((), (), s32[]{:S(2)}) async-start(), calls=%async_computation.17 | async-start | bytes 1179648 | tf_op jit(solution)/shard_map/all_gather | solution.py:227
  137.9 305.5 %all-gather.35.cloned.1.call-start = ((), (), s32[]{:S(2)}) async-start(), calls=%async_computation.20 | async-start | bytes 4718592 | tf_op jit(solution)/shard_map/all_gather | solution.py:238
  138.6 338.4 %all-gather.37.cloned.1.call-start = ((), (), s32[]{:S(2)}) async-start(), calls=%async_computation.21 | async-start | bytes 4718592 | tf_op jit(solution)/shard_map/all_gather | solution.py:239
  139.2 371.6 %all-gather.39.cloned.1.call-start = ((), (), s32[]{:S(2)}) async-start(), calls=%async_computation.22 | async-start | bytes 4718592 | tf_op jit(solution)/shard_map/all_gather | solution.py:240
  140.0 611.4 %reduce-scatter.17.cloned.1.call-start = ((), (), s32[]{:S(2)}) async-start(), calls=%async_computation.23 | async-start | bytes 2228224 | tf_op jit(solution)/shard_map/reduce_scatter | solution.py:620
  681.1 239.0 %all-gather.45.cloned.1.call-start = ((), (), s32[]{:S(2)}) async-start(), calls=%async_computation.38 | async-start | bytes 13369344 | tf_op jit(solution)/shard_map/all_gather | solution.py:41
  689.5 322.4 %all-gather.47.cloned.1.call-start = ((), (), s32[]{:S(2)}) async-start(), calls=%async_computation.39 | async-start | bytes 13369344 | tf_op jit(solution)/shard_map/all_gather | solution.py:41
  691.3 432.5 %reduce-scatter.21.cloned.1.call-start = ((), (), s32[]{:S(2)}) async-start(), calls=%async_computation.25 | async-start | bytes 2359296 | tf_op jit(solution)/shard_map/reduce_scatter | solution.py:663
  694.9 428.9 %reduce-scatter.27.cloned.1.call-start = ((), (), s32[]{:S(2)}) async-start(), calls=%async_computation.28 | async-start | bytes 2359296 | tf_op jit(solution)/shard_map/reduce_scatter | solution.py:666
  697.8 426.1 %reduce-scatter.23.cloned.1.call-start = ((), (), s32[]{:S(2)}) async-start(), calls=%async_computation.26 | async-start | bytes 589824 | tf_op jit(solution)/shard_map/reduce_scatter | solution.py:664
  753.6 392.9 %reduce-scatter.25.cloned.1.call-start = ((), (), s32[]{:S(2)}) async-start(), calls=%async_computation.27 | async-start | bytes 589824 | tf_op jit(solution)/shard_map/reduce_scatter | solution.py:665
  830.9 359.2 %reduce-scatter.35.cloned.1.call-start = ((), (), s32[]{:S(2)}) async-start(), calls=%async_computation.32 | async-start | bytes 7077888 | tf_op jit(solution)/shard_map/reduce_scatter | solution.py:675
  835.8 408.8 %reduce-scatter.37.cloned.1.call-start = ((), (), s32[]{:S(2)}) async-start(), calls=%async_computation.33 | async-start | bytes 9437184 | tf_op jit(solution)/shard_map/reduce_scatter | solution.py:677
  842.7 456.5 %reduce-scatter.39.cloned.1.call-start = ((), (), s32[]{:S(2)}) async-start(), calls=%async_computation.34 | async-start | bytes 9437184 | tf_op jit(solution)/shard_map/reduce_scatter | solution.py:678
  848.6 505.0 %reduce-scatter.41.cloned.1.call-start = ((), (), s32[]{:S(2)}) async-start(), calls=%async_computation.35 | async-start | bytes 9437184 | tf_op jit(solution)/shard_map/reduce_scatter | solution.py:679
  855.6 532.4 %reduce-scatter.31.cloned.1.call-start = ((), (), s32[]{:S(2)}) async-start(), calls=%async_computation.30 | async-start | bytes 1179648 | tf_op jit(solution)/shard_map/reduce_scatter | solution.py:668
  1106.3 355.4 %reduce-scatter.29.cloned.1.call-start = ((), (), s32[]{:S(2)}) async-start(), calls=%async_computation.29 | async-start | bytes 14155776 | tf_op jit(solution)/shard_map/reduce_scatter | solution.py:667
  1114.1 391.1 %reduce-scatter.43.cloned.1.call-start = ((), (), s32[]{:S(2)}) async-start(), calls=%async_computation.40 | async-start | bytes 1032192
  1122.4 405.3 %reduce-scatter.33.cloned.1.call-start = ((), (), s32[]{:S(2)}) async-start(), calls=%async_computation.31 | async-start | bytes 110592 | tf_op jit(solution)/shard_map/reduce_scatter | solution.py:669
  1123.4 532.9 %all-reduce.34.cloned.1.call-start = ((), (), s32[]{:S(2)}) async-start(), calls=%async_computation.41 | async-start | bytes 12582912 | tf_op jit(solution)/shard_map/psum | solution.py:681
  (246 other events, 6084.4 us)
Sparse Core Ops, SparseCore 0:
  9.7 44.9 all-gather.30
  82.9 43.4 all-gather.24
  128.9 42.1 all-gather.26
  173.6 89.3 all-gather.40
  265.7 89.7 all-gather.42
  411.4 31.9 all-gather.34
  445.0 32.0 all-gather.36
  478.8 32.0 all-gather.38
  676.9 74.4 reduce-scatter.16
  755.0 73.6 reduce-scatter.18
  830.8 89.2 all-gather.44
  922.1 89.7 all-gather.46
  1014.1 33.2 reduce-scatter.20
  1049.6 32.4 reduce-scatter.26
  1084.3 29.7 reduce-scatter.22
  1116.7 29.8 reduce-scatter.24
  1148.8 41.2 reduce-scatter.34
  1192.5 52.1 reduce-scatter.36
  1247.1 52.0 reduce-scatter.38
  1301.6 52.0 reduce-scatter.40
  1356.4 31.4 reduce-scatter.30
  1390.4 71.1 reduce-scatter.28
  1464.4 31.1 reduce-scatter.42
  1532.5 123.8 all-reduce.33
  (4 shorter events, 103.3 us)
where the time goes:
time: 1690 us; the launch traced here: 1680 us
  waiting for transfers between devices  849 us (50%)
  matrix products  248 us (15%)
  blocking collectives  237 us (14%)
  other arithmetic  196 us (12%)
  local copies, waits for them, and re-layouts  90.1 us (5%)
  between operations  24.1 us (1%)
  loops' own time  22.2 us (1%)
    all_gather x4, waiting for transfers between devices, carried_in(): gathered = jax.tree.map(lambda a: lax.all_gather(a, axis), part)  224 us
    add x30, other arithmetic, compose(): later[0][:, None, None] * earlier[1] + later[1]  88.7 us
    dot_general x19, matrix products, left_product(): lax.dot_general(left, right, (((0,), (0,)), ((), ())), preferred_element_...  76.8 us
    psum x1, blocking collectives, local(): lax.psum((shards_out[0], shards_out[1], shards_out[2], shards_out[3], sha...  76 us
    reduce_scatter x1, waiting for transfers between devices, local(): lax.psum_scatter(d_values, 'ctx', scatter_dimension=0, tiled=True)  75.1 us
    reduce_scatter x1, waiting for transfers between devices, local(): lax.psum_scatter(gradients[5], 'fsdp', scatter_dimension=0, tiled=True)  73.6 us
    dot_general x23, matrix products, right_product(): lax.dot_general(left, right, (((1,), (1,)), ((), ())), preferred_element_...  69.2 us
    reduce_scatter x1, waiting for transfers between devices, local(): lax.psum_scatter(gradients[15], 'fsdp', scatter_dimension=0, tiled=True)  54.6 us
  transfers between devices with their start and end apart: 32, of which 21 were waited for; matrix products, arithmetic and copies ran while one was open for 21% of the time, Pallas kernels for 0%

commit v1 on v0

v1 whole, which is shorter than its diff:
```python
import jax
import jax.numpy as jnp
from jax import lax
from jax.experimental import pallas as pl
from jax.experimental.pallas import tpu as pltpu
from jax.sharding import PartitionSpec as P

HEADS = 8
KV_HEADS = 2
HEAD_DIM = 64
MIX_HEADS = 24
MIX_DIM = 64
STATE = 128
CONV = 4
QW = 512
KW = 128
MIX = 1536
CH = 1792
LB = 128
SMALL = 11


EPSILON = 1e-05
ROPE_BASE = 100000000000.0
HIGHEST = lax.Precision.HIGHEST
NEG_LARGE = -1e30


def product(left, right):
    return jnp.dot(left, right, preferred_element_type=jnp.float32)


def left_product(left, right):
    return lax.dot_general(
        left, right, (((0,), (0,)), ((), ())), preferred_element_type=jnp.float32
    )


def right_product(left, right):
    return lax.dot_general(
        left, right, (((1,), (1,)), ((), ())), preferred_element_type=jnp.float32
    )


def rms_scale(values, gain_vector):
    return (
        values
        * lax.rsqrt(jnp.mean(values * values, axis=-1, keepdims=True) + EPSILON)
        * gain_vector
    )


def rope_tables(places):
    half_dim = HEAD_DIM // 2
    inverse = ROPE_BASE ** (-jnp.arange(half_dim, dtype=jnp.float32) / half_dim)
    angles = places.astype(jnp.float32)[:, None] * inverse[None, :]
    return (jnp.tile(jnp.cos(angles), (1, 4)), jnp.tile(jnp.sin(angles), (1, 4)))


def swap_matrix(width):
    row = lax.broadcasted_iota(jnp.int32, (width, width), 0)
    col = lax.broadcasted_iota(jnp.int32, (width, width), 1)
    half_dim = HEAD_DIM // 2
    lower = col % HEAD_DIM < half_dim
    return jnp.where(
        lower & (row == col + half_dim),
        -1.0,
        jnp.where(~lower & (row == col - half_dim), 1.0, 0.0),
    ).astype(jnp.float32)


def rotate(values, cosine, sine_part, sign):
    width = values.shape[1]
    swapped = jnp.dot(values, swap_matrix(width), precision=HIGHEST)
    repeats = width // cosine.shape[1]
    return values * jnp.tile(cosine, (1, repeats)) + sign * swapped * jnp.tile(
        sine_part, (1, repeats)
    )


WIDE = HEADS * LB


def split_heads(rows, target, half):
    turned = jnp.transpose(rows.astype(jnp.float32))
    zeros = jnp.zeros((HEAD_DIM, LB), target.dtype)
    for head in range(HEADS):
        group = head // (HEADS // KV_HEADS)
        cols = slice(head * LB, (head + 1) * LB)
        own = slice(group * HEAD_DIM, (group + 1) * HEAD_DIM)
        other = slice((1 - group) * HEAD_DIM, (2 - group) * HEAD_DIM)
        target[half, own, cols] = turned[head * HEAD_DIM : (head + 1) * HEAD_DIM].astype(
            target.dtype
        )
        target[half, other, cols] = zeros


def join_heads(wide):
    pieces = []
    for head in range(HEADS):
        group = head // (HEADS // KV_HEADS)
        pieces.append(
            wide[group * HEAD_DIM : (group + 1) * HEAD_DIM, head * LB : (head + 1) * LB]
        )
    return jnp.transpose(jnp.concatenate(pieces, axis=0))


def block_mask(rows_ref, block, half):
    base = jnp.where(half == 0, block, 31 - block) * LB
    key_at = lax.broadcasted_iota(jnp.int32, (LB, WIDE), 0) + base
    return (key_at <= rows_ref[half, 0:1, :]) & (key_at >= rows_ref[half, 1:2, :])


def pair_at(step, own):
    half = (step >= own).astype(jnp.int32)
    return step + half, half


def transposed_dot(left, right):
    return lax.dot_general(
        left, right, (((0,), (0,)), ((), ())), preferred_element_type=jnp.float32
    )


def attend_kernel(own_ref, rows_ref, query_ref, kv_ref, out_ref, log_ref, turned, total, peak, mass):
    own = own_ref[0]
    for half in range(2):
        scaled = query_ref[half * LB : (half + 1) * LB, :] * 0.125
        split_heads(scaled, turned, half)

    def scores(block, half):
        at = pl.multiple_of(half * LB, LB)
        keys = kv_ref[block, pl.ds(at, LB), 0:KW]
        values = kv_ref[block, pl.ds(at, LB), KW : 2 * KW]
        found = product(keys, turned[half])
        return jnp.where(block_mask(rows_ref, block, half), found, NEG_LARGE), values

    for half in range(2):
        found, values = scores(own, half)
        top = jnp.max(found, axis=0, keepdims=True)
        weights = jnp.exp(found - top)
        peak[half] = top
        mass[half] = jnp.sum(weights, axis=0, keepdims=True)
        total[half] = transposed_dot(values, weights.astype(jnp.bfloat16))

    def one(step, carry):
        block, half = pair_at(step, own)
        found, values = scores(block, half)
        old = peak[half]
        top = jnp.maximum(old, jnp.max(found, axis=0, keepdims=True))
        fade = jnp.exp(old - top)
        weights = jnp.exp(found - top)
        peak[half] = top
        mass[half] = mass[half] * fade + jnp.sum(weights, axis=0, keepdims=True)
        total[half] = total[half] * fade + transposed_dot(values, weights.astype(jnp.bfloat16))
        return carry

    lax.fori_loop(0, kv_ref.shape[0] - 1, one, 0)
    for half in range(2):
        out_ref[half * LB : (half + 1) * LB, :] = join_heads(total[half] / mass[half]).astype(
            out_ref.dtype
        )
        log_ref[half] = peak[half] + jnp.log(mass[half])


def attend_back_kernel(
    own_ref,
    rows_ref,
    query_ref,
    kv_ref,
    out_ref,
    log_ref,
    up_ref,
    d_query_ref,
    d_kv_ref,
    turned,
    turned_up,
    inner,
    total,
):
    own = own_ref[0]
    d_kv_ref[...] = jnp.zeros(d_kv_ref.shape, d_kv_ref.dtype)
    for half in range(2):
        rows = slice(half * LB, (half + 1) * LB)
        split_heads(query_ref[rows, :] * 0.125, turned, half)
        split_heads(up_ref[rows, :], turned_up, half)
        both = jnp.transpose(out_ref[rows, :].astype(jnp.float32) * up_ref[rows, :].astype(jnp.float32))
        for head in range(HEADS):
            inner[half, :, head * LB : (head + 1) * LB] = jnp.sum(
                both[head * HEAD_DIM : (head + 1) * HEAD_DIM], axis=0, keepdims=True
            )
        total[half] = jnp.zeros((KW, WIDE), jnp.float32)

    def visit(block, half):
        at = pl.multiple_of(half * LB, LB)
        keys = kv_ref[block, pl.ds(at, LB), 0:KW]
        values = kv_ref[block, pl.ds(at, LB), KW : 2 * KW]
        found = product(keys, turned[half])
        weights = jnp.where(
            block_mask(rows_ref, block, half), jnp.exp(found - log_ref[half]), 0.0
        )
        d_weights = product(values, turned_up[half])
        d_scores = (weights * (d_weights - inner[half])).astype(jnp.bfloat16)
        total[half] += transposed_dot(keys, d_scores)
        d_kv_ref[block, pl.ds(at, LB), 0:KW] = right_product(d_scores, turned[half]).astype(
            d_kv_ref.dtype
        )
        d_kv_ref[block, pl.ds(at, LB), KW : 2 * KW] = right_product(
            weights.astype(jnp.bfloat16), turned_up[half]
        ).astype(d_kv_ref.dtype)

    visit(own, 0)
    visit(own, 1)

    def one(step, carry):
        block, half = pair_at(step, own)
        visit(block, half)
        return carry

    lax.fori_loop(0, kv_ref.shape[0] - 1, one, 0)
    for half in range(2):
        d_query_ref[half * LB : (half + 1) * LB, :] = join_heads(total[half]) * 0.125


VMEM_SPEC = pl.BlockSpec(memory_space=pltpu.VMEM)
SMEM_SPEC = pl.BlockSpec(memory_space=pltpu.SMEM)


def attend(own, rows, queries, kv_all):
    return pl.pallas_call(
        attend_kernel,
        out_shape=(
            jax.ShapeDtypeStruct((2 * LB, QW), jnp.bfloat16),
            jax.ShapeDtypeStruct((2, 1, WIDE), jnp.float32),
        ),
        in_specs=[SMEM_SPEC, VMEM_SPEC, VMEM_SPEC, VMEM_SPEC],
        out_specs=(VMEM_SPEC, VMEM_SPEC),
        scratch_shapes=[
            pltpu.VMEM((2, KW, WIDE), jnp.bfloat16),
            pltpu.VMEM((2, KW, WIDE), jnp.float32),
            pltpu.VMEM((2, 1, WIDE), jnp.float32),
            pltpu.VMEM((2, 1, WIDE), jnp.float32),
        ],
        compiler_params=pltpu.CompilerParams(vmem_limit_bytes=32 * 1024 * 1024),
        cost_estimate=pl.CostEstimate(
            flops=17 * 4 * LB * KW * WIDE, bytes_accessed=3 * 2**20, transcendentals=17 * LB * WIDE
        ),
        name="attend",
    )(own, rows, queries, kv_all)


def attend_back(own, rows, queries, kv_all, attended, logs, upstream):
    return pl.pallas_call(
        attend_back_kernel,
        out_shape=(
            jax.ShapeDtypeStruct((2 * LB, QW), jnp.float32),
            jax.ShapeDtypeStruct(kv_all.shape, jnp.bfloat16),
        ),
        in_specs=[SMEM_SPEC] + [VMEM_SPEC] * 6,
        out_specs=(VMEM_SPEC, VMEM_SPEC),
        scratch_shapes=[
            pltpu.VMEM((2, KW, WIDE), jnp.bfloat16),
            pltpu.VMEM((2, KW, WIDE), jnp.bfloat16),
            pltpu.VMEM((2, 1, WIDE), jnp.float32),
            pltpu.VMEM((2, KW, WIDE), jnp.float32),
        ],
        compiler_params=pltpu.CompilerParams(vmem_limit_bytes=32 * 1024 * 1024),
        cost_estimate=pl.CostEstimate(
            flops=17 * 10 * LB * KW * WIDE, bytes_accessed=6 * 2**20, transcendentals=17 * LB * WIDE
        ),
        name="attend_back",
    )(own, rows, queries, kv_all, attended, logs, upstream)


PAIRS = MIX_HEADS // 2
PAIR = 2 * MIX_DIM


def lane_is_low():
    return lax.broadcasted_iota(jnp.int32, (LB, PAIR), 1) < MIX_DIM


def spread_pair(columns, pair, low_lanes):
    return jnp.where(
        low_lanes, columns[:, 2 * pair : 2 * pair + 1], columns[:, 2 * pair + 1 : 2 * pair + 2]
    )


def low_dot(left, right, left_dim, right_dim):
    return lax.dot_general(
        left.astype(jnp.bfloat16),
        right.astype(jnp.bfloat16),
        (((left_dim,), (right_dim,)), ((), ())),
        preferred_element_type=jnp.float32,
    )


def exact_dot(left, right):
    return jnp.dot(left, right, precision=HIGHEST, preferred_element_type=jnp.float32)


def triangle(lower):
    row = lax.broadcasted_iota(jnp.int32, (LB, LB), 0)
    col = lax.broadcasted_iota(jnp.int32, (LB, LB), 1)
    return jnp.where(col <= row if lower else col >= row, 1.0, 0.0).astype(jnp.float32)


def softplus(values):
    return jnp.maximum(values, 0.0) + jnp.log1p(jnp.exp(-jnp.abs(values)))


def sigmoid(values):
    return 1.0 / (1.0 + jnp.exp(-values))


def block_base(own, half):
    return (own if half == 0 else 31 - own) * LB


def stage_rows(pre_ref, stage, half):
    edge = 2 * LB + 8 * half
    cols = slice(2 * KW, 2 * KW + CH)
    stage[0:8, :] = pre_ref[edge : edge + 8, cols].astype(jnp.bfloat16).astype(jnp.float32)
    stage[8 : 8 + LB, :] = (
        pre_ref[half * LB : (half + 1) * LB, cols].astype(jnp.bfloat16).astype(jnp.float32)
    )


def window(stage, starts, base, offset):
    back = CONV - 1 - offset
    at = lax.broadcasted_iota(jnp.int32, (LB, 1), 0) + base - back
    keep = jnp.where(at >= starts, 1.0, 0.0)
    return stage[8 - back : 8 - back + LB, :] * keep


def mix_in_kernel(
    own_ref, pre_ref, starts_ref, taps_ref, shift_ref, heads_ref, conv_ref, step_ref, sum_ref,
    state_ref, decay_ref, stage
):
    own = own_ref[0]
    low_lanes = lane_is_low()
    lower = triangle(True)
    for half in range(2):
        rows = slice(half * LB, (half + 1) * LB)
        base = block_base(own, half)
        starts = starts_ref[rows, 0:1]
        stage_rows(pre_ref, stage, half)
        total = jnp.zeros((LB, CH), jnp.float32) + shift_ref[0:1, :]
        for offset in range(CONV):
            total = total + taps_ref[offset : offset + 1, :] * window(stage, starts, base, offset)
        conv_ref[rows, :] = (total * sigmoid(total)).astype(jnp.bfloat16)
        step = softplus(pre_ref[rows, 2 * KW + CH :] + heads_ref[0:1, :])
        summed = exact_dot(lower, -step * jnp.exp(heads_ref[1:2, :]))
        step_ref[rows, :] = step
        sum_ref[rows, :] = summed
        last = summed[LB - 1 : LB, :]
        same = starts == starts[LB - 1 : LB, :]
        weight = jnp.where(same, jnp.exp(last - summed), 0.0) * step
        decay_ref[half : half + 1, :] = jnp.where(
            starts[LB - 1 : LB, :] < base, jnp.exp(last), 0.0
        )
        write = conv_ref[rows, MIX : MIX + STATE]
        for pair in range(PAIRS):
            cols = slice(pair * PAIR, (pair + 1) * PAIR)
            driven = conv_ref[rows, cols].astype(jnp.float32) * spread_pair(weight, pair, low_lanes)
            state_ref[half, cols, :] = low_dot(driven, write, 0, 0).astype(jnp.bfloat16)


def block_terms(conv_ref, step_ref, sum_ref, starts_ref, rows, base):
    starts = starts_ref[rows, 0:1]
    summed = sum_ref[rows, :]
    step = step_ref[rows, :]
    summed_t = jnp.transpose(summed)
    step_t = jnp.transpose(step)
    row = lax.broadcasted_iota(jnp.int32, (LB, LB), 0)
    col = lax.broadcasted_iota(jnp.int32, (LB, LB), 1)
    allowed = (col <= row) & (col + base >= starts)
    write = conv_ref[rows, MIX : MIX + STATE]
    read = conv_ref[rows, MIX + STATE :]
    inner = low_dot(read, write, 1, 1)
    carried = jnp.where(starts < base, jnp.exp(summed), 0.0)
    return summed, step, summed_t, step_t, allowed, write, read, inner, carried


def head_decay(summed, summed_t, allowed, head):
    spread = summed[:, head : head + 1] - summed_t[head : head + 1, :]
    return jnp.exp(jnp.where(allowed, spread, NEG_LARGE))


def mix_out_kernel(
    own_ref, conv_ref, step_ref, sum_ref, starts_ref, skip_ref, entry_ref, gate_ref,
    scan_ref, gated_ref
):
    own = own_ref[0]
    low_lanes = lane_is_low()
    for half in range(2):
        rows = slice(half * LB, (half + 1) * LB)
        summed, step, summed_t, step_t, allowed, write, read, inner, carried = block_terms(
            conv_ref, step_ref, sum_ref, starts_ref, rows, block_base(own, half)
        )
        for pair in range(PAIRS):
            cols = slice(pair * PAIR, (pair + 1) * PAIR)
            values = conv_ref[rows, cols]
            found = []
            for head in (2 * pair, 2 * pair + 1):
                mixing = (
                    head_decay(summed, summed_t, allowed, head) * inner * step_t[head : head + 1, :]
                )
                found.append(low_dot(mixing, values, 1, 0))
            total = jnp.where(low_lanes, found[0], found[1])
            total = total + spread_pair(carried, pair, low_lanes) * low_dot(
                read, entry_ref[half, cols, :], 1, 1
            )
            total = total + skip_ref[0:1, cols] * values.astype(jnp.float32)
            gate = gate_ref[rows, cols].astype(jnp.float32)
            scan_ref[rows, cols] = total
            gated_ref[rows, cols] = (total * gate * sigmoid(gate)).astype(jnp.bfloat16)


def mix_back_kernel(
    own_ref, conv_ref, step_ref, sum_ref, starts_ref, skip_ref, entry_ref, gate_ref, scan_ref,
    up_ref, d_gate_ref, d_values_ref, d_entry_ref, d_keys_ref, d_sum_ref, d_step_ref, d_skip_ref,
    row_a, row_b
):
    own = own_ref[0]
    low_lanes = lane_is_low()
    lane = lax.broadcasted_iota(jnp.int32, (LB, LB), 1)
    row_a[...] = jnp.zeros(row_a.shape, jnp.float32)
    row_b[...] = jnp.zeros(row_b.shape, jnp.float32)
    for half in range(2):
        rows = slice(half * LB, (half + 1) * LB)
        summed, step, summed_t, step_t, allowed, write, read, inner, carried = block_terms(
            conv_ref, step_ref, sum_ref, starts_ref, rows, block_base(own, half)
        )
        d_inner = jnp.zeros((LB, LB), jnp.float32)
        d_read = jnp.zeros((LB, STATE), jnp.float32)
        d_sum = jnp.zeros((LB, LB), jnp.float32)
        for pair in range(PAIRS):
            cols = slice(pair * PAIR, (pair + 1) * PAIR)
            values = conv_ref[rows, cols]
            values32 = values.astype(jnp.float32)
            gate = gate_ref[rows, cols].astype(jnp.float32)
            sig = sigmoid(gate)
            up = up_ref[rows, cols].astype(jnp.float32)
            d_scan = up * gate * sig
            d_gate_ref[rows, cols] = (
                up * scan_ref[rows, cols] * sig * (1.0 + gate * (1.0 - sig))
            ).astype(jnp.bfloat16)
            d_skip_ref[half : half + 1, cols] = jnp.sum(d_scan * values32, axis=0, keepdims=True)
            d_values = skip_ref[0:1, cols] * d_scan
            entry = entry_ref[half, cols, :]
            through = low_dot(read, entry, 1, 1) * d_scan
            for place in range(2):
                head = 2 * pair + place
                own_lanes = low_lanes if place == 0 else jnp.logical_not(low_lanes)
                d_own = jnp.where(own_lanes, d_scan, 0.0).astype(jnp.bfloat16)
                decay = head_decay(summed, summed_t, allowed, head)
                step_row = step_t[head : head + 1, :]
                raw = low_dot(d_own, values, 1, 1) * decay
                scaled = raw * step_row
                d_inner = d_inner + scaled
                mixed = decay * inner * step_row
                d_values = d_values + low_dot(mixed, d_own, 0, 0)
                kept = raw * inner
                by_key = jnp.sum(kept, axis=0, keepdims=True)
                row_a[head : head + 1, :] = by_key
                row_b[head : head + 1, :] = by_key * step_row
                by_row = jnp.sum(scaled * inner, axis=1, keepdims=True) + carried[
                    :, head : head + 1
                ] * jnp.sum(jnp.where(own_lanes, through, 0.0), axis=1, keepdims=True)
                d_sum = d_sum + jnp.where(lane == head, by_row, 0.0)
            d_values_ref[rows, cols] = d_values
            d_carry = (d_scan * spread_pair(carried, pair, low_lanes)).astype(jnp.bfloat16)
            d_read = d_read + low_dot(d_carry, entry, 1, 0)
            d_entry_ref[half, cols, :] = low_dot(d_carry, read, 0, 0).astype(jnp.bfloat16)
        d_keys_ref[rows, 0:STATE] = low_dot(d_inner, read, 0, 0)
        d_keys_ref[rows, STATE:] = d_read + low_dot(d_inner, write, 1, 0)
        d_sum_ref[rows, :] = d_sum - jnp.transpose(row_b[...])
        d_step_ref[rows, :] = jnp.transpose(row_a[...])


def mix_end_kernel(
    own_ref, conv_ref, step_ref, sum_ref, starts_ref, pre_ref, taps_ref, shift_ref, heads_ref,
    decay_ref, entry_ref, after_ref, d_values_ref, d_keys_ref, d_sum_ref, d_step_ref,
    d_own_ref, d_pre_ref, d_taps_ref, d_heads_ref, stage, d_stage, d_conv, meet, edges
):
    own = own_ref[0]
    low_lanes = lane_is_low()
    lane = lax.broadcasted_iota(jnp.int32, (LB, LB), 1)
    upper = triangle(False)
    rate = jnp.exp(heads_ref[1:2, :])
    d_pre_ref[0 : 2 * LB, 0 : 2 * KW] = d_own_ref[...]
    quiet = jnp.zeros((16, 2 * KW), d_pre_ref.dtype)
    d_pre_ref[2 * LB :, 0 : 2 * KW] = quiet
    d_pre_ref[2 * LB :, 2 * KW + CH :] = quiet[:, 0:128]
    meet[...] = jnp.zeros(meet.shape, jnp.float32)
    d_taps_ref[...] = jnp.zeros(d_taps_ref.shape, jnp.float32)
    d_heads_ref[...] = jnp.zeros(d_heads_ref.shape, jnp.float32)
    for half in range(2):
        rows = slice(half * LB, (half + 1) * LB)
        base = block_base(own, half)
        starts = starts_ref[rows, 0:1]
        summed = sum_ref[rows, :]
        step = step_ref[rows, :]
        last = summed[LB - 1 : LB, :]
        same = starts == starts[LB - 1 : LB, :]
        fade = jnp.where(same, jnp.exp(last - summed), 0.0)
        weight = fade * step
        write = conv_ref[rows, MIX : MIX + STATE]
        d_write = jnp.zeros((LB, STATE), jnp.float32)
        d_weight = jnp.zeros((LB, LB), jnp.float32)
        for pair in range(PAIRS):
            cols = slice(pair * PAIR, (pair + 1) * PAIR)
            values = conv_ref[rows, cols].astype(jnp.float32)
            after = after_ref[half, cols, :]
            reach = low_dot(write, after, 1, 1)
            wide = spread_pair(weight, pair, low_lanes)
            d_conv[:, cols] = d_values_ref[rows, cols] + wide * reach
            d_write = d_write + low_dot(values * wide, after, 1, 0)
            both = values * reach
            overlap = after.astype(jnp.float32) * entry_ref[half, cols, :].astype(jnp.float32)
            for place in range(2):
                head = 2 * pair + place
                own_lanes = low_lanes if place == 0 else jnp.logical_not(low_lanes)
                column = jnp.sum(jnp.where(own_lanes, both, 0.0), axis=1, keepdims=True)
                d_weight = d_weight + jnp.where(lane == head, column, 0.0)
                meet[head : head + 1, :] = jnp.sum(
                    overlap[place * MIX_DIM : (place + 1) * MIX_DIM], axis=0, keepdims=True
                )
        d_conv[:, MIX : MIX + STATE] = d_keys_ref[rows, 0:STATE] + d_write
        d_conv[:, MIX + STATE :] = d_keys_ref[rows, STATE:]
        met = jnp.sum(jnp.transpose(meet[...]), axis=0, keepdims=True)
        moved = d_weight * weight
        d_last = (
            jnp.sum(moved, axis=0, keepdims=True) + decay_ref[half : half + 1, :] * met
        )
        at_last = lax.broadcasted_iota(jnp.int32, (LB, LB), 0) == LB - 1
        d_sum = d_sum_ref[rows, :] - moved + jnp.where(at_last, d_last, 0.0)
        d_rate = exact_dot(upper, d_sum)
        d_step = d_step_ref[rows, :] + d_weight * fade - d_rate * rate
        raw = pre_ref[rows, 2 * KW + CH :] + heads_ref[0:1, :]
        d_raw = jnp.where(lane < MIX_HEADS, d_step * sigmoid(raw), 0.0)
        d_heads_ref[0:1, :] += jnp.sum(d_raw, axis=0, keepdims=True)
        d_heads_ref[1:2, :] += jnp.sum(-d_rate * step * rate, axis=0, keepdims=True)
        d_pre_ref[rows, 2 * KW + CH :] = d_raw.astype(d_pre_ref.dtype)
        stage_rows(pre_ref, stage, half)
        total = jnp.zeros((LB, CH), jnp.float32) + shift_ref[0:1, :]
        for offset in range(CONV):
            total = total + taps_ref[offset : offset + 1, :] * window(stage, starts, base, offset)
        sig = sigmoid(total)
        d_total = d_conv[...] * sig * (1.0 + total * (1.0 - sig))
        d_taps_ref[CONV : CONV + 1, :] += jnp.sum(d_total, axis=0, keepdims=True)
        d_stage[...] = jnp.zeros(d_stage.shape, jnp.float32)
        for offset in range(CONV):
            back = CONV - 1 - offset
            at = lax.broadcasted_iota(jnp.int32, (LB, 1), 0) + base - back
            keep = jnp.where(at >= starts, 1.0, 0.0)
            kept = d_total * keep
            seen = stage[8 - back : 8 - back + LB, :]
            d_taps_ref[offset : offset + 1, :] += jnp.sum(kept * seen, axis=0, keepdims=True)
            d_stage[8 - back : 8 - back + LB, :] += taps_ref[offset : offset + 1, :] * kept
        edges[8 * half : 8 * half + 8, :] = d_stage[0:8, :]
        d_pre_ref[rows, 2 * KW : 2 * KW + CH] = d_stage[8 : 8 + LB, :].astype(d_pre_ref.dtype)
    d_pre_ref[2 * LB :, 2 * KW : 2 * KW + CH] = edges[...].astype(d_pre_ref.dtype)


def kernel_call(kernel, name, shapes, scratch, inputs):
    outs = tuple(jax.ShapeDtypeStruct(shape, dtype) for shape, dtype in shapes)
    moved = sum(value.size * value.dtype.itemsize for value in inputs) + sum(
        out.size * out.dtype.itemsize for out in outs
    )
    return pl.pallas_call(
        kernel,
        out_shape=outs,
        in_specs=[SMEM_SPEC] + [VMEM_SPEC] * (len(inputs) - 1),
        out_specs=tuple(VMEM_SPEC for _ in outs),
        scratch_shapes=[pltpu.VMEM(shape, dtype) for shape, dtype in scratch],
        compiler_params=pltpu.CompilerParams(vmem_limit_bytes=40 * 1024 * 1024),
        cost_estimate=pl.CostEstimate(
            flops=2 * 10**9, bytes_accessed=moved, transcendentals=10**6
        ),
        name=name,
    )(*inputs)


def ring_up(values):
    count = lax.axis_size("ctx")
    return lax.ppermute(values, "ctx", [(i, i + 1) for i in range(count - 1)])


def ring_down(values):
    count = lax.axis_size("ctx")
    return lax.ppermute(values, "ctx", [(i + 1, i) for i in range(count - 1)])


def gather(shard):
    return lax.all_gather(shard, "fsdp", axis=0, tiled=True)


def scatter(total):
    return lax.psum_scatter(total.astype(jnp.bfloat16), "fsdp", scatter_dimension=0, tiled=True)


def exchange(values):
    return lax.all_to_all(values, "ctx", 0, 0, tiled=True)


def spread(values, axis):
    count = lax.axis_size(axis)
    copies = jnp.broadcast_to(values[None], (count,) + values.shape)
    return lax.all_to_all(copies, axis, 0, 0, tiled=True)


def added(pieces):
    return jnp.sum(pieces.astype(jnp.float32), axis=0).astype(jnp.bfloat16)


def sum_ctx(shard):
    parts = lax.axis_size("ctx")
    pieces = exchange(shard.reshape((parts, -1) + shard.shape[1:]))
    return spread(added(pieces), "ctx").reshape(shard.shape)


def gather_across(shard):
    parts = lax.axis_size("ctx")
    count = shard.shape[0] // parts
    own = lax.dynamic_slice_in_dim(shard, lax.axis_index("ctx") * count, count, 0)
    whole = spread(spread(own, "fsdp"), "ctx")
    return whole.transpose(1, 0, 2, 3).reshape(-1, shard.shape[1])


def sum_across(total):
    parts = lax.axis_size("ctx")
    shards = lax.axis_size("fsdp")
    width = total.shape[1]
    pieces = total.reshape(shards, parts, -1, width).transpose(1, 0, 2, 3)
    held = added(exchange(pieces))
    held = added(lax.all_to_all(held, "fsdp", 0, 0, tiled=True))
    return spread(held, "ctx").reshape(-1, width)


def pack_small(parts, rows):
    flat = jnp.concatenate([part.reshape(-1) for part in parts])
    flat = jnp.pad(flat, (0, rows * SMALL - flat.shape[0]))
    return flat.reshape(rows, SMALL)


def small_sizes(shards):
    return (1024 // shards, CONV * CH // shards, CH // shards) + (MIX_HEADS // shards,) * 3 + (
        1024 // shards,
    )


def split_small(flat, shards):
    pieces = []
    start = 0
    for size in small_sizes(shards):
        pieces.append(flat[..., start : start + size])
        start += size
    return pieces


def head_rows(values, parts):
    return jnp.repeat(values, MIX_DIM, axis=-1).reshape(values.shape[0], parts, -1)


def send_states(states, parts):
    halves = states.shape[0]
    shaped = states.astype(jnp.bfloat16).reshape(halves, parts, MIX // parts, STATE)
    return shaped.transpose(1, 0, 2, 3)


def running(factors, states, ahead):
    count = states.shape[0]
    order = list(range(count)) if ahead else list(range(count - 1, -1, -1))
    found = [None] * count
    state = jnp.zeros_like(states[0])
    for place in order:
        found[place] = state
        state = factors[place][:, None] * state + states[place]
    return jnp.stack(found)


def local(
    tokens,
    cotangent,
    lengths,
    input_gain,
    query_weight,
    key_weight,
    value_weight,
    attention_out,
    mixer_in,
    state_in,
    step_in,
    conv_weight,
    conv_bias,
    step_bias,
    decay_log,
    skip_gain,
    mixer_out,
    feed_gain,
    gate_weight,
    up_weight,
    down_weight,
):
    shards = lax.axis_size("fsdp")
    parts = lax.axis_size("ctx")
    ctx_index = lax.axis_index("ctx")
    rows = input_gain.shape[0]
    small = pack_small(
        (input_gain, conv_weight, conv_bias, step_bias, decay_log, skip_gain, feed_gain), rows
    )
    pad_cols = 128 - MIX_HEADS - SMALL
    first_proj = gather(
        jnp.concatenate(
            [
                key_weight,
                value_weight,
                mixer_in[:, MIX:],
                state_in,
                step_in,
                small,
                jnp.zeros((rows, pad_cols), jnp.bfloat16),
            ],
            axis=1,
        )
    )
    second_proj = gather(jnp.concatenate([query_weight, mixer_in[:, :MIX]], axis=1))
    out_proj = gather(jnp.concatenate([attention_out, mixer_out], axis=0))
    gate_up_proj = gather(jnp.concatenate([gate_weight, up_weight], axis=1))
    down_proj = gather_across(down_weight)
    step_at = 2 * KW + CH
    small_at = step_at + MIX_HEADS
    small_all = first_proj[:, small_at : small_at + SMALL].astype(jnp.float32).reshape(shards, -1)
    gain_in32, taps32, shift32, step_shift32, decay32, skip32, feed32 = split_small(
        small_all, shards
    )
    gain_in32 = gain_in32.reshape(-1)
    taps32 = taps32.reshape(shards, CONV, -1).transpose(1, 0, 2).reshape(CONV, CH)
    shift32 = shift32.reshape(-1)
    step_shift32 = step_shift32.reshape(-1)
    decay32 = decay32.reshape(-1)
    skip32 = skip32.reshape(-1)
    feed32 = feed32.reshape(-1)

    row_count = tokens.shape[1]
    half_rows = row_count // 2
    first_start = ctx_index * half_rows
    second_start = (2 * parts - 1 - ctx_index) * half_rows
    offsets = jnp.arange(half_rows, dtype=jnp.int32)
    places = jnp.concatenate([first_start + offsets, second_start + offsets])
    bounds = jnp.cumsum(lengths[0])
    doc_starts = jnp.max(
        jnp.where(bounds[None, :-1] <= places[:, None], bounds[None, :-1], 0), axis=1
    )
    row_limits = jnp.tile(
        jnp.stack([places, doc_starts]).reshape(2, 2, half_rows).transpose(1, 0, 2), (1, 1, HEADS)
    )
    own = ctx_index.reshape(1).astype(jnp.int32)
    cosine, sine_part = rope_tables(places)

    x_own = tokens[0]
    x_ext = jnp.concatenate(
        [x_own, ring_up(x_own[half_rows - 8 : half_rows]), ring_down(x_own[row_count - 8 :])]
    ).astype(jnp.float32)
    normed_ext = rms_scale(x_ext, gain_in32).astype(jnp.bfloat16)
    normed = normed_ext[:row_count]
    first_pre = product(normed_ext, first_proj)
    keys_rot = rotate(first_pre[:row_count, :KW], cosine, sine_part, 1.0).astype(jnp.bfloat16)
    values_low = first_pre[:row_count, KW : 2 * KW].astype(jnp.bfloat16)
    kv_all = spread(jnp.concatenate([keys_rot, values_low], axis=1), "ctx")
    starts_col = jnp.broadcast_to(doc_starts[:, None], (row_count, 128)).astype(jnp.int32)
    pad_heads = 128 - MIX_HEADS
    head_terms = jnp.pad(jnp.stack([step_shift32, decay32]), ((0, 6), (0, pad_heads)))
    taps_pad = jnp.pad(taps32, ((0, 4), (0, 0)))
    shift_row = shift32[None]
    skip_row = jnp.repeat(skip32, MIX_DIM)[None]
    conv_out, steps, sums, states, block_decay = kernel_call(
        mix_in_kernel,
        "mix_in",
        (
            ((row_count, CH), jnp.bfloat16),
            ((row_count, 128), jnp.float32),
            ((row_count, 128), jnp.float32),
            ((2, MIX, STATE), jnp.bfloat16),
            ((2, 128), jnp.float32),
        ),
        (((LB + 8, CH), jnp.float32),),
        (own, first_pre, starts_col, taps_pad, shift_row, head_terms),
    )

    decay_rows = head_rows(block_decay[:, :MIX_HEADS], parts).transpose(1, 0, 2)
    decay_high = decay_rows.astype(jnp.bfloat16)
    decay_low = (decay_rows - decay_high.astype(jnp.float32)).astype(jnp.bfloat16)
    decay_both = jnp.stack([decay_high, decay_low], axis=2)
    decay_both = jnp.pad(decay_both, ((0, 0), (0, 0), (0, 14), (0, STATE - MIX // parts)))
    states_out = send_states(states, parts)
    seen = exchange(jnp.concatenate([states_out, decay_both], axis=2)).astype(jnp.float32)
    slice_rows = MIX // parts
    seen_states = seen[:, :, :slice_rows]
    seen_decay = (seen[:, :, slice_rows] + seen[:, :, slice_rows + 1])[:, :, :slice_rows]
    entries = jnp.stack(
        [
            running(seen_decay[:, 0], seen_states[:, 0], True),
            running(seen_decay[:, 1], seen_states[:, 1], False),
        ],
        axis=1,
    ).astype(jnp.bfloat16)
    entries = exchange(entries).transpose(1, 0, 2, 3).reshape(2, MIX, STATE)

    second_pre = product(normed, second_proj)
    queries = rotate(second_pre[:, :QW], cosine, sine_part, 1.0).astype(jnp.bfloat16)
    gate_z = second_pre[:, QW:].astype(jnp.bfloat16)
    attended_low, log_totals = attend(own, row_limits, queries, kv_all)

    scanned, gated_low = kernel_call(
        mix_out_kernel,
        "mix_out",
        (((row_count, MIX), jnp.float32), ((row_count, MIX), jnp.bfloat16)),
        (),
        (own, conv_out, steps, sums, starts_col, skip_row, entries, gate_z),
    )
    x_rows = x_ext[:row_count]
    out_split = out_proj.reshape(shards, -1, out_proj.shape[1])
    attn_proj = out_split[:, : QW // shards].reshape(QW, -1)
    mix_proj = out_split[:, QW // shards :].reshape(MIX, -1)
    middle = x_rows + product(attended_low, attn_proj) + product(gated_low, mix_proj)
    normed_ff = rms_scale(middle, feed32).astype(jnp.bfloat16)
    gate_up = product(normed_ff, gate_up_proj)
    width = gate_up.shape[1] // 2
    gate_vals = gate_up[:, :width]
    up_vals = gate_up[:, width:]
    activ = (jax.nn.silu(gate_vals) * up_vals).astype(jnp.bfloat16)
    output = (middle + product(activ, down_proj)).astype(jnp.bfloat16)

    grad_out = cotangent[0]
    d_activ = right_product(grad_out, down_proj)
    d_down_own = sum_across(left_product(activ, grad_out).astype(jnp.bfloat16))
    sig_gate = jax.nn.sigmoid(gate_vals)
    d_gate = d_activ * up_vals * sig_gate * (1.0 + gate_vals * (1.0 - sig_gate))
    d_up = d_activ * gate_vals * sig_gate
    d_gate_up = jnp.concatenate([d_gate, d_up], axis=1).astype(jnp.bfloat16)
    d_gate_up_shard = scatter(left_product(normed_ff, d_gate_up))
    d_normed_ff = right_product(d_gate_up, gate_up_proj)
    _, feed_pull = jax.vjp(rms_scale, middle, feed32)
    d_middle_norm, d_feed_gain = feed_pull(d_normed_ff)
    d_middle = grad_out.astype(jnp.float32) + d_middle_norm
    d_middle_low = d_middle.astype(jnp.bfloat16)
    d_out_total = jnp.concatenate(
        [
            left_product(attended_low, d_middle_low)
            .astype(jnp.bfloat16)
            .reshape(shards, QW // shards, -1),
            left_product(gated_low, d_middle_low)
            .astype(jnp.bfloat16)
            .reshape(shards, MIX // shards, -1),
        ],
        axis=1,
    )
    d_out_shard = scatter(d_out_total.reshape(QW + MIX, -1))
    d_attended = right_product(d_middle_low, attn_proj).astype(jnp.bfloat16)
    d_gated = right_product(d_middle_low, mix_proj).astype(jnp.bfloat16)

    d_queries, d_kv = attend_back(
        own, row_limits, queries, kv_all, attended_low, log_totals, d_attended
    )
    d_kv_own = jnp.sum(exchange(d_kv).astype(jnp.float32), axis=0)
    d_query_pre = rotate(d_queries, cosine, sine_part, -1.0).astype(jnp.bfloat16)

    d_gate_z, d_values_part, d_entries, d_keys_part, d_sums, d_steps, d_skip_cols = kernel_call(
        mix_back_kernel,
        "mix_back",
        (
            ((row_count, MIX), jnp.bfloat16),
            ((row_count, MIX), jnp.float32),
            ((2, MIX, STATE), jnp.bfloat16),
            ((row_count, 2 * STATE), jnp.float32),
            ((row_count, 128), jnp.float32),
            ((row_count, 128), jnp.float32),
            ((2, MIX), jnp.float32),
        ),
        (((128, 128), jnp.float32), ((128, 128), jnp.float32)),
        (own, conv_out, steps, sums, starts_col, skip_row, entries, gate_z, scanned, d_gated),
    )
    d_second = jnp.concatenate([d_query_pre, d_gate_z], axis=1)
    d_second_shard = scatter(left_product(normed, d_second))
    seen_back = exchange(send_states(d_entries, parts)).astype(jnp.float32)
    afters = jnp.stack(
        [
            running(seen_decay[:, 0], seen_back[:, 0], False),
            running(seen_decay[:, 1], seen_back[:, 1], True),
        ],
        axis=1,
    ).astype(jnp.bfloat16)
    afters = exchange(afters).transpose(1, 0, 2, 3).reshape(2, MIX, STATE)
    d_key_pre = rotate(d_kv_own[:, :KW], cosine, sine_part, -1.0)
    d_first_own = jnp.concatenate([d_key_pre, d_kv_own[:, KW:]], axis=1).astype(jnp.bfloat16)
    d_first, d_taps_all, d_heads = kernel_call(
        mix_end_kernel,
        "mix_end",
        (
            ((row_count + 16, step_at + 128), jnp.bfloat16),
            ((8, CH), jnp.float32),
            ((8, 128), jnp.float32),
        ),
        (
            ((LB + 8, CH), jnp.float32),
            ((LB + 8, CH), jnp.float32),
            ((LB, CH), jnp.float32),
            ((128, 128), jnp.float32),
            ((16, CH), jnp.float32),
        ),
        (
            own,
            conv_out,
            steps,
            sums,
            starts_col,
            first_pre,
            taps_pad,
            shift_row,
            head_terms,
            block_decay,
            entries,
            afters,
            d_values_part,
            d_keys_part,
            d_sums,
            d_steps,
            d_first_own,
        ),
    )
    d_step_shift = d_heads[0, :MIX_HEADS]
    d_decay = d_heads[1, :MIX_HEADS]
    d_skip = d_skip_cols.sum(axis=0).reshape(MIX_HEADS, MIX_DIM).sum(axis=1)
    d_normed = right_product(d_first, first_proj) + jnp.pad(
        right_product(d_second, second_proj), ((0, 16), (0, 0))
    )
    _, input_pull = jax.vjp(rms_scale, x_ext, gain_in32)
    d_rows_norm, d_input_gain = input_pull(d_normed)
    edge_low = ring_down(d_rows_norm[row_count : row_count + 8])
    edge_high = ring_up(d_rows_norm[row_count + 8 :])
    input_grad = d_middle + d_rows_norm[:row_count]
    input_grad = input_grad.at[half_rows - 8 : half_rows].add(edge_low)
    input_grad = input_grad.at[row_count - 8 :].add(edge_high)[None]

    d_taps = (
        d_taps_all[:CONV].reshape(CONV, shards, -1).transpose(1, 0, 2)
    )
    d_small = jnp.concatenate(
        [
            piece.reshape(shards, -1)
            for piece in (
                d_input_gain,
                d_taps,
                d_taps_all[CONV],
                d_step_shift,
                d_decay,
                d_skip,
                d_feed_gain,
            )
        ],
        axis=1,
    )
    d_small = jnp.pad(d_small, ((0, 0), (0, rows * SMALL - d_small.shape[1])))
    d_first_total = left_product(normed_ext, d_first).astype(jnp.bfloat16)
    d_first_total = lax.dynamic_update_slice(
        d_first_total, d_small.reshape(shards * rows, SMALL).astype(jnp.bfloat16), (0, small_at)
    )
    d_first_own, d_second_own, d_out_own, d_gate_up_own, d_down_own = (
        total.astype(jnp.float32)
        for total in (
            sum_ctx(scatter(d_first_total)),
            sum_ctx(d_second_shard),
            sum_ctx(d_out_shard),
            sum_ctx(d_gate_up_shard),
            d_down_own,
        )
    )
    grad_gain, grad_taps, grad_shift, grad_step, grad_decay, grad_skip, grad_feed = split_small(
        d_first_own[:, small_at : small_at + SMALL].reshape(-1), shards
    )
    attn_rows = QW // shards
    return (
        output[None],
        input_grad,
        grad_gain,
        d_second_own[:, :QW],
        d_first_own[:, :KW],
        d_first_own[:, KW : 2 * KW],
        d_out_own[:attn_rows],
        jnp.concatenate([d_second_own[:, QW:], d_first_own[:, 2 * KW : 2 * KW + MIX]], axis=1),
        d_first_own[:, 2 * KW + MIX : step_at],
        d_first_own[:, step_at:small_at],
        grad_taps.reshape(CONV, -1),
        grad_shift,
        grad_step,
        grad_decay,
        grad_skip,
        d_out_own[attn_rows:],
        grad_feed,
        d_gate_up_own[:, :width],
        d_gate_up_own[:, width:],
        d_down_own,
    )


def solution(mesh):
    return jax.shard_map(
        local,
        mesh=mesh,
        in_specs=(
            P("fsdp", "ctx", None),
            P("fsdp", "ctx", None),
            P("fsdp", None),
            P("fsdp"),
            P("fsdp", None),
            P("fsdp", None),
            P("fsdp", None),
            P("fsdp", None),
            P("fsdp", None),
            P("fsdp", None),
            P("fsdp", None),
            P(None, "fsdp"),
            P("fsdp"),
            P("fsdp"),
            P("fsdp"),
            P("fsdp"),
            P("fsdp", None),
            P("fsdp"),
            P("fsdp", None),
            P("fsdp", None),
            P("fsdp", None),
        ),
        out_specs=(
            P("fsdp", "ctx", None),
            P("fsdp", "ctx", None),
            P("fsdp"),
            P("fsdp", None),
            P("fsdp", None),
            P("fsdp", None),
            P("fsdp", None),
            P("fsdp", None),
            P("fsdp", None),
            P("fsdp", None),
            P(None, "fsdp"),
            P("fsdp"),
            P("fsdp"),
            P("fsdp"),
            P("fsdp"),
            P("fsdp", None),
            P("fsdp"),
            P("fsdp", None),
            P("fsdp", None),
            P("fsdp", None),
        ),
        check_vma=False,
    )
```

time: 1690 us -> 601 us (0.36)
  waiting for transfers between devices: 849 us -> 155 us
  matrix products: 248 us -> 65.5 us
  other arithmetic: 196 us -> 37.4 us
  blocking collectives: 237 us -> 108 us
  starting transfers between devices: 10.5 us -> 80 us
  Pallas kernels: 0 us -> 55.8 us
  loops' own time: 22.2 us -> 0 us
  local copies, waits for them, and re-layouts: 90.1 us -> 70.4 us
    reduce_scatter x13 -> x4, waiting for transfers between devices: 488 us -> 0.03 us  [scatter(): lax.psum_scatter(total.astype(jnp.bfloat16), 'fsdp', scatter_dimension=0,...]
    all_gather x13 -> x4, waiting for transfers between devices: 294 us -> 23.5 us  [gather(): return lax.all_gather(shard, 'fsdp', axis=0, tiled=True)]
    all_to_all x0 -> x14, waiting for transfers between devices: none -> 131 us  [the longest x8 66.8 us: exchange(): return lax.all_to_all(values, 'ctx', 0, 0, tiled=True)]
    all_gather x9 -> x0, blocking collectives: 125 us -> none  [the longest x2 43.7 us: carried_in(): gathered = jax.tree.map(lambda a: lax.all_gather(a, axis), part)]
    all_to_all x0 -> x5, blocking collectives: none -> 108 us  [the longest x2 67.7 us: exchange(): return lax.all_to_all(values, 'ctx', 0, 0, tiled=True)]
    add x47 -> x2, other arithmetic: 92.7 us -> 2.87 us  [the longest x1 2.85 us: local(): input_grad = d_middle + d_rows_norm[:row_count]]
    psum x1 -> x0, blocking collectives: 76 us -> none  [local(): lax.psum((shards_out[0], shards_out[1], shards_out[2], shards_out[3], sha...]
    all_to_all x0 -> x14, starting transfers between devices: none -> 68.1 us  [the longest x8 37.9 us: exchange(): return lax.all_to_all(values, 'ctx', 0, 0, tiled=True)]
  transfers between devices with their start and end apart: 32 -> 26, of which waited for: 21 -> 13; matrix products, arithmetic and copies ran while one was open for 21% -> 22% of each run, Pallas kernels for 0% -> 9%
where the time goes in v1:
time: 601 us; the launch traced here: 590 us
  waiting for transfers between devices  155 us (26%)
  blocking collectives  108 us (18%)
  starting transfers between devices  80 us (13%)
  local copies, waits for them, and re-layouts  70.4 us (12%)
  matrix products  65.5 us (11%)
  Pallas kernels  55.8 us (9%)
  other arithmetic  37.4 us (6%)
  between operations  17.6 us (3%)
    all_to_all x2, blocking collectives, exchange(): return lax.all_to_all(values, 'ctx', 0, 0, tiled=True)  67.7 us
    all_to_all x8, waiting for transfers between devices, exchange(): return lax.all_to_all(values, 'ctx', 0, 0, tiled=True)  66.8 us
    all_to_all x6, waiting for transfers between devices, spread(): return lax.all_to_all(copies, axis, 0, 0, tiled=True)  64.4 us
    all_to_all x8, starting transfers between devices, exchange(): return lax.all_to_all(values, 'ctx', 0, 0, tiled=True)  37.9 us
    all_to_all x6, starting transfers between devices, spread(): return lax.all_to_all(copies, axis, 0, 0, tiled=True)  30.2 us
    pallas_call x4, Pallas kernels, kernel_call(): pl.pallas_call(kernel, out_shape=outs, in_specs=[SMEM_SPEC] + [VMEM_SPEC]...  30 us
    all_to_all x2, blocking collectives, spread(): return lax.all_to_all(copies, axis, 0, 0, tiled=True)  28.2 us
    all_gather x4, waiting for transfers between devices, gather(): return lax.all_gather(shard, 'fsdp', axis=0, tiled=True)  23.5 us
  transfers between devices with their start and end apart: 26, of which 13 were waited for; matrix products, arithmetic and copies ran while one was open for 22% of the time, Pallas kernels for 9%

profile of v1, /device:TPU:0, one launch (start us, length us, event | category | flops | bytes accessed | tf_op | source)
XLA Modules:
  0.0 589.7 jit_solution(1710393447880092521)
XLA Ops:
  31.4 23.5 %all-gather.5.cloned.1.call-done = bf16[1024,2176]{1,0:T(8,128)(2,1)} async-done(((bf16[128,2176]{1,0:T(8,128)(2,1)}), bf16[1024,2176]{1,0:T(8,128)(2,1)}) %all-gather.5.cloned.1.call-update) | async-done | bytes 4456464 | tf_op jit(solution)/shard_map/all_gather | solution.py:597
  70.0 7.0 %all-to-all-start.1 = ((bf16[16,2,112,128]{3,1,2,0:T(2,128)(2,1)}), bf16[16,2,112,128]{3,1,2,0:T(2,128)(2,1)}, u32[]{:S(2)}, u32[]{:S(2)}) async-start(bf16[16,2,112,128]{3,1,2,0:T(2,128)(2,1)} %fusion.18), calls=%async_computation.1 | async-start | bytes 1835008 | tf_op jit(solution)/shard_map/all_to_all | solution.py:605
  78.2 15.5 %all-to-all-done.1 = bf16[16,2,112,128]{3,1,2,0:T(2,128)(2,1)} async-done(((bf16[16,2,112,128]{3,1,2,0:T(2,128)(2,1)}), bf16[16,2,112,128]{3,1,2,0:T(2,128)(2,1)}, u32[]{:S(2)}, u32[]{:S(2)}) %all-to-all-start.1) | async-done | bytes 917536 | tf_op jit(solution)/shard_map/all_to_all | solution.py:605
  107.9 47.0 %all-to-all-done.4 = bf16[16,8,16,1024]{3,2,1,0:T(8,128)(2,1)} async-done(((bf16[16,8,16,1024]{3,2,1,0:T(8,128)(2,1)}), bf16[16,8,16,1024]{3,2,1,0:T(8,128)(2,1)}, u32[]{:S(2)}, u32[]{:S(2)}) %all-to-all-start.4) | async-done | bytes 4194336 | tf_op jit(solution)/shard_map/all_to_all | solution.py:611
  164.8 5.9 %all-to-all-done.2 = bf16[16,2,96,128]{3,2,1,0:T(8,128)(2,1)} async-done(((bf16[16,2,96,128]{3,2,1,0:T(8,128)(2,1)}), bf16[16,2,96,128]{3,2,1,0:T(8,128)(2,1)}, u32[]{:S(2)}, u32[]{:S(2)}) %all-to-all-start.2) | async-done | bytes 786464 | tf_op jit(solution)/shard_map/all_to_all | solution.py:605
  202.9 11.0 %attend.1 = (bf16[256,512]{1,0:T(8,128)(2,1)S(1)}, f32[2,1,1024]{2,1,0:T(1,128)S(1)}) custom-call(s32[1]{0:T(128)} %bitcast.3.own_ref, s32[2,2,1024]{2,1,0:T(2,128)S(1)} %tile.21.rows_ref, bf16[256,512]{1,0:T(8,128)(2,1)S(1)} %copy-done.28, bf16[16,256,256]{2,1,0:T(8,128)(2,1)} %all-to-all-done.kv_ref), custom_call_target="tpu_custom_call" | custom-call | flops 1140850688 | bytes 3145728 | tf_op jit(solution)/shard_map/attend/pallas_call | solution.py:230
  217.2 6.2 %fusion.176 = f32[256,4096]{1,0:T(8,128)S(1)} fusion(bf16[1024,4096]{1,0:T(8,128)(2,1)} %all-gather.11.cloned.1.call-done, f32[256,1024]{1,0:T(8,128)} %get-tuple-element.215, f32[1024]{0:T(1024)S(1)} %get-tuple-element.264, f32[256]{0:T(256)S(1)} %fusion.150), kind=kOutput, calls=%fused_computation.434 | convolution fusion | flops 2148270080 | bytes 13636608 | tf_op jit(solution)/shard_map/dot_general | solution.py:30
  238.5 15.0 %mix_back.1 = (bf16[256,1536]{1,0:T(8,128)(2,1)S(1)}, f32[256,1536]{1,0:T(8,128)S(1)}, bf16[2,1536,128]{2,1,0:T(8,128)(2,1)S(1)}, f32[256,256]{1,0:T(8,128)S(1)}...) custom-call(s32[1]{0:T(128)} %bitcast.3.own_ref, bf16[256,1792]{1,0:T(8,128)(2,1)S(1)} %copy-done.7, ...), custom_call_target="tpu_custom_call" | custom-call | flops 2000000000 | bytes 8931332 | tf_op jit(solution)/shard_map/mix_back/pallas_call | solution.py:572
  255.8 6.9 %all-to-all-start.5 = ((bf16[16,2,96,128]{3,2,1,0:T(8,128)(2,1)}), bf16[16,2,96,128]{3,2,1,0:T(8,128)(2,1)}, u32[]{:S(2)}, u32[]{:S(2)}) async-start(bf16[16,2,96,128]{3,2,1,0:T(8,128)(2,1)} %bitcast.681), calls=%async_computation.5 | async-start | bytes 1572864 | tf_op jit(solution)/shard_map/all_to_all | solution.py:605
  264.6 14.8 %attend_back.1 = (f32[256,512]{1,0:T(8,128)S(1)}, bf16[16,256,256]{2,1,0:T(8,128)(2,1)}) custom-call(s32[1]{0:T(128)} %bitcast.3.own_ref, s32[2,2,1024]{2,1,0:T(2,128)S(1)} %tile.21.rows_ref, bf16[256,512]{1,0:T(8,128)(2,1)S(1)} %copy-done.29, bf16[16,256,256]{2,1,0:T(8,128)(2,1)} %all-to-all-done.kv_ref, bf16[256,512]{1,0:T(8,128)(2,1)S(1)} %get-tuple-element.65.out_ref, ...), custom_call_target="tpu_custom_call" | custom-call | flops 2852126720 | bytes 6291456 | tf_op jit(solution)/shard_map/attend_back/pallas_call | solution.py:253
  288.6 18.4 %all_to_all.95 = bf16[16,2,96,128]{3,2,1,0:T(8,128)(2,1)} all-to-all(bf16[16,2,96,128]{3,2,1,0:T(8,128)(2,1)S(1)} %copy.244), channel_id=1, replica_groups=mesh['ctx'=16,'fsdp'=8] {'ctx'}, dimensions={0} | all-to-all | bytes 1572864 | tf_op jit(solution)/shard_map/all_to_all | solution.py:605
  317.1 16.7 %all-to-all-done.7 = bf16[16,256,256]{2,1,0:T(8,128)(2,1)} async-done(((bf16[16,256,256]{2,1,0:T(8,128)(2,1)}), bf16[16,256,256]{2,1,0:T(8,128)(2,1)}, u32[]{:S(2)}, u32[]{:S(2)}) %all-to-all-start.7) | async-done | bytes 2097184 | tf_op jit(solution)/shard_map/all_to_all | solution.py:605
  339.6 8.3 %mix_end.1 = (bf16[272,2176]{1,0:T(8,128)(2,1)S(1)}, f32[8,1792]{1,0:T(8,128)S(1)}, f32[8,128]{1,0:T(8,128)S(1)}) custom-call(s32[1]{0:T(128)} %bitcast.3.own_ref, bf16[256,1792]{1,0:T(8,128)(2,1)S(1)} %copy-done.7, f32[256,128]{1,0:T(8,128)S(1)} %copy-done.16, f32[256,128]{1,0:T(8,128)S(1)} %copy-done.19, s32[256,128]{1,0:T(8,128)S(1)} %broadcast_in_dim.135.starts_ref, ...), custom_call_target="tpu_custom_call" | custom-call | flops 2000000000 | bytes 8794116 | tf_op jit(solution)/shard_map/mix_end/pallas_call | solution.py:572
  349.5 5.8 multiply_reduce_fusion
  365.0 7.0 %convolution_convert_fusion = bf16[1024,4096]{1,0:T(8,128)(2,1)} fusion(bf16[256,2048]{1,0:T(8,128)(2,1)} %copy-done.59, bf16[256,2048]{1,0:T(8,128)(2,1)S(1)} %copy-done.58, f32[256,1024]{1,0:T(8,128)S(1)} %copy-done.31, f32[1024]{0:T(1024)S(1)} %get-tuple-element.264, f32[256]{0:T(256)S(1)} %fusion.150), kind=kOutput, calls=%fused_computation | convolution fusion | flops 2156658688 | bytes 11539456 | tf_op jit(solution)/shard_map/dot_general | solution.py:34
  375.5 49.3 %all_to_all.96 = bf16[16,8,16,1024]{3,2,1,0:T(8,128)(2,1)} all-to-all(bf16[16,8,16,1024]{3,2,1,0:T(8,128)(2,1)S(1)} %bitcast.663), channel_id=1, replica_groups=mesh['ctx'=16,'fsdp'=8] {'ctx'}, dimensions={0} | all-to-all | bytes 8388608 | tf_op jit(solution)/shard_map/all_to_all | solution.py:605
  428.1 12.1 %all_to_all.97 = bf16[8,16,1024]{2,1,0:T(8,128)(2,1)S(1)} all-to-all(bf16[8,16,1024]{2,1,0:T(8,128)(2,1)S(1)} %reduce_sum.190), channel_id=1, replica_groups=mesh['ctx'=16,'fsdp'=8] {'fsdp'}, dimensions={0} | all-to-all | bytes 524288 | tf_op jit(solution)/shard_map/all_to_all | solution.py:638
  440.3 14.9 %all_to_all.98 = bf16[16,16,1024]{2,1,0:T(8,128)(2,1)} all-to-all(bf16[16,16,1024]{2,1,0:T(8,128)(2,1)S(1)} %broadcast_in_dim.149), channel_id=1, replica_groups=mesh['ctx'=16,'fsdp'=8] {'ctx'}, dimensions={0} | all-to-all | bytes 1048576 | tf_op jit(solution)/shard_map/all_to_all | solution.py:611
  458.8 10.3 %all-to-all-done.12 = bf16[16,16,1024]{2,1,0:T(8,128)(2,1)S(1)} async-done(((bf16[16,16,1024]{2,1,0:T(8,128)(2,1)}), bf16[16,16,1024]{2,1,0:T(8,128)(2,1)S(1)}, u32[]{:S(2)}, u32[]{:S(2)}) %all-to-all-start.12) | async-done | bytes 524320 | tf_op jit(solution)/shard_map/all_to_all | solution.py:605
  472.7 10.0 %all-to-all-done.10 = bf16[16,8,2048]{2,1,0:T(8,128)(2,1)S(1)} async-done(((bf16[16,8,2048]{2,1,0:T(8,128)(2,1)}), bf16[16,8,2048]{2,1,0:T(8,128)(2,1)S(1)}, u32[]{:S(2)}, u32[]{:S(2)}) %all-to-all-start.10) | async-done | bytes 524320 | tf_op jit(solution)/shard_map/all_to_all | solution.py:605
  482.7 13.4 %all_to_all.99 = bf16[16,16,1024]{2,1,0:T(8,128)(2,1)S(1)} all-to-all(bf16[16,16,1024]{2,1,0:T(8,128)(2,1)S(1)} %broadcast_in_dim.147), channel_id=1, replica_groups=mesh['ctx'=16,'fsdp'=8] {'ctx'}, dimensions={0} | all-to-all | bytes 1048576 | tf_op jit(solution)/shard_map/all_to_all | solution.py:611
  526.0 8.5 %all-to-all-start.9 = ((bf16[16,8,2176]{2,1,0:T(8,128)(2,1)}), bf16[16,8,2176]{2,1,0:T(8,128)(2,1)S(1)}, u32[]{:S(2)}, u32[]{:S(2)}) async-start(bf16[16,8,2176]{2,1,0:T(8,128)(2,1)} %broadcast_in_dim.145), calls=%async_computation.10 | async-start | bytes 1114112 | tf_op jit(solution)/shard_map/all_to_all | solution.py:611
  536.7 8.0 %all-to-all-done.9 = bf16[16,8,2176]{2,1,0:T(8,128)(2,1)S(1)} async-done(((bf16[16,8,2176]{2,1,0:T(8,128)(2,1)}), bf16[16,8,2176]{2,1,0:T(8,128)(2,1)S(1)}, u32[]{:S(2)}, u32[]{:S(2)}) %all-to-all-start.9) | async-done | bytes 557088 | tf_op jit(solution)/shard_map/all_to_all | solution.py:611
  572.4 8.6 %all-to-all-done.15 = bf16[16,8,4096]{2,1,0:T(8,128)(2,1)S(1)} async-done(((bf16[16,8,4096]{2,1,0:T(8,128)(2,1)}), bf16[16,8,4096]{2,1,0:T(8,128)(2,1)S(1)}, u32[]{:S(2)}, u32[]{:S(2)}) %all-to-all-start.15) | async-done | bytes 1048608 | tf_op jit(solution)/shard_map/all_to_all | solution.py:611
  (639 shorter events, 227.8 us)
Async XLA Ops:
  7.2 47.6 %all-gather.5.cloned.1.call-start = ((), (), s32[]{:S(2)}) async-start(), calls=%async_computation.23 | async-start | bytes 5013504 | tf_op jit(solution)/shard_map/all_gather | solution.py:597
  16.2 167.2 %all-gather.9.cloned.1.call-start = ((), (), s32[]{:S(2)}) async-start(), calls=%async_computation.25 | async-start | bytes 4718592 | tf_op jit(solution)/shard_map/all_gather | solution.py:597
  17.2 172.7 %all-gather.7.cloned.1.call-start = ((), (), s32[]{:S(2)}) async-start(), calls=%async_computation.24 | async-start | bytes 4718592 | tf_op jit(solution)/shard_map/all_gather | solution.py:597
  24.1 45.9 %all-to-all-start.3 = ((bf16[8,16,1024]{2,1,0:T(8,128)(2,1)}), bf16[8,16,1024]{2,1,0:T(8,128)(2,1)}, u32[]{:S(2)}, u32[]{:S(2)}) async-start(bf16[8,16,1024]{2,1,0:T(8,128)(2,1)} %broadcast_in_dim.138), calls=%async_computation.3 | async-start | bytes 524288 | tf_op jit(solution)/shard_map/all_to_all | solution.py:611
  28.6 188.6 %all-gather.11.cloned.1.call-start = ((), (), s32[]{:S(2)}) async-start(), calls=%async_computation.26 | async-start | bytes 9437184 | tf_op jit(solution)/shard_map/all_gather | solution.py:597
  70.0 23.7 %all-to-all-start.1 = ((bf16[16,2,112,128]{3,1,2,0:T(2,128)(2,1)}), bf16[16,2,112,128]{3,1,2,0:T(2,128)(2,1)}, u32[]{:S(2)}, u32[]{:S(2)}) async-start(bf16[16,2,112,128]{3,1,2,0:T(2,128)(2,1)} %fusion.18), calls=%async_computation.1 | async-start | bytes 1835008 | tf_op jit(solution)/shard_map/all_to_all | solution.py:605
  97.2 57.8 %all-to-all-start.4 = ((bf16[16,8,16,1024]{3,2,1,0:T(8,128)(2,1)}), bf16[16,8,16,1024]{3,2,1,0:T(8,128)(2,1)}, u32[]{:S(2)}, u32[]{:S(2)}) async-start(bf16[16,8,16,1024]{3,2,1,0:T(8,128)(2,1)} %broadcast_in_dim.139), calls=%async_computation.4 | async-start | bytes 8388608 | tf_op jit(solution)/shard_map/all_to_all | solution.py:611
  154.9 15.8 %all-to-all-start.2 = ((bf16[16,2,96,128]{3,2,1,0:T(8,128)(2,1)}), bf16[16,2,96,128]{3,2,1,0:T(8,128)(2,1)}, u32[]{:S(2)}, u32[]{:S(2)}) async-start(bf16[16,2,96,128]{3,2,1,0:T(8,128)(2,1)} %copy.239), calls=%async_computation.2 | async-start | bytes 1572864 | tf_op jit(solution)/shard_map/all_to_all | solution.py:605
  172.3 29.7 %all-to-all-start = ((bf16[16,256,256]{2,1,0:T(8,128)(2,1)}), bf16[16,256,256]{2,1,0:T(8,128)(2,1)}, u32[]{:S(2)}, u32[]{:S(2)}) async-start(bf16[16,256,256]{2,1,0:T(8,128)(2,1)} %broadcast_in_dim.134), calls=%async_computation | async-start | bytes 4194304 | tf_op jit(solution)/shard_map/all_to_all | solution.py:611
  177.1 278.1 %reduce-scatter.9.cloned.1.call-start = ((), (), s32[]{:S(2)}) async-start(), calls=%async_computation.29 | async-start | bytes 4718592 | tf_op jit(solution)/shard_map/reduce_scatter | solution.py:601
  255.8 28.6 %all-to-all-start.5 = ((bf16[16,2,96,128]{3,2,1,0:T(8,128)(2,1)}), bf16[16,2,96,128]{3,2,1,0:T(8,128)(2,1)}, u32[]{:S(2)}, u32[]{:S(2)}) async-start(bf16[16,2,96,128]{3,2,1,0:T(8,128)(2,1)} %bitcast.681), calls=%async_computation.5 | async-start | bytes 1572864 | tf_op jit(solution)/shard_map/all_to_all | solution.py:605
  262.8 196.0 %reduce-scatter.7.cloned.1.call-start = ((), (), s32[]{:S(2)}) async-start(), calls=%async_computation.28 | async-start | bytes 4718592 | tf_op jit(solution)/shard_map/reduce_scatter | solution.py:601
  307.0 26.8 %all-to-all-start.7 = ((bf16[16,256,256]{2,1,0:T(8,128)(2,1)}), bf16[16,256,256]{2,1,0:T(8,128)(2,1)}, u32[]{:S(2)}, u32[]{:S(2)}) async-start(bf16[16,256,256]{2,1,0:T(8,128)(2,1)} %get-tuple-element.79), calls=%async_computation.7 | async-start | bytes 4194304 | tf_op jit(solution)/shard_map/all_to_all | solution.py:605
  311.6 184.5 %reduce-scatter.5.cloned.1.call-start = ((), (), s32[]{:S(2)}) async-start(), calls=%async_computation.27 | async-start | bytes 5013504 | tf_op jit(solution)/shard_map/reduce_scatter | solution.py:601
  363.5 181.3 %reduce-scatter.11.cloned.1.call-start = ((), (), s32[]{:S(2)}) async-start(), calls=%async_computation.30 | async-start | bytes 9437184 | tf_op jit(solution)/shard_map/reduce_scatter | solution.py:601
  455.2 13.9 %all-to-all-start.12 = ((bf16[16,16,1024]{2,1,0:T(8,128)(2,1)}), bf16[16,16,1024]{2,1,0:T(8,128)(2,1)S(1)}, u32[]{:S(2)}, u32[]{:S(2)}) async-start(bf16[16,16,1024]{2,1,0:T(8,128)(2,1)} %bitcast.693), calls=%async_computation.15 | async-start | bytes 1048576 | tf_op jit(solution)/shard_map/all_to_all | solution.py:605
  469.0 13.6 %all-to-all-start.10 = ((bf16[16,8,2048]{2,1,0:T(8,128)(2,1)}), bf16[16,8,2048]{2,1,0:T(8,128)(2,1)S(1)}, u32[]{:S(2)}, u32[]{:S(2)}) async-start(bf16[16,8,2048]{2,1,0:T(8,128)(2,1)} %bitcast.694), calls=%async_computation.12 | async-start | bytes 1048576 | tf_op jit(solution)/shard_map/all_to_all | solution.py:605
  496.1 13.8 %all-to-all-start.8 = ((bf16[16,8,2176]{2,1,0:T(8,128)(2,1)}), bf16[16,8,2176]{2,1,0:T(8,128)(2,1)S(1)}, u32[]{:S(2)}, u32[]{:S(2)}) async-start(bf16[16,8,2176]{2,1,0:T(8,128)(2,1)} %bitcast.686), calls=%async_computation.9 | async-start | bytes 1114112 | tf_op jit(solution)/shard_map/all_to_all | solution.py:605
  510.8 14.4 %all-to-all-start.11 = ((bf16[16,8,2048]{2,1,0:T(8,128)(2,1)}), bf16[16,8,2048]{2,1,0:T(8,128)(2,1)}, u32[]{:S(2)}, u32[]{:S(2)}) async-start(bf16[16,8,2048]{2,1,0:T(8,128)(2,1)} %broadcast_in_dim.146), calls=%async_computation.13 | async-start | bytes 1048576 | tf_op jit(solution)/shard_map/all_to_all | solution.py:611
  515.8 18.7 %collective-permute-start.2 = (f32[8,1024]{1,0:T(8,128)S(1)}, f32[8,1024]{1,0:T(8,128)S(1)}, u32[]{:S(2)}, u32[]{:S(2)}) collective-permute-start(f32[8,1024]{1,0:T(8,128)S(1)} %get-tuple-element.259), channel_id=1, source_target_pairs={{8,0},{16,8},{24,16},{32,24},{40,32},{48,40},{56,48},{64,56},{72,6... | collective-permute-start | bytes 98312 | tf_op jit(solution)/shard_map/ppermute | solution.py:593
  520.0 14.7 %collective-permute-start.3 = (f32[8,1024]{1,0:T(8,128)S(1)}, f32[8,1024]{1,0:T(8,128)S(1)}, u32[]{:S(2)}, u32[]{:S(2)}) collective-permute-start(f32[8,1024]{1,0:T(8,128)S(1)} %get-tuple-element.258), channel_id=1, source_target_pairs={{0,8},{8,16},{16,24},{24,32},{32,40},{40,48},{48,56},{56,64},{64,7... | collective-permute-start | bytes 98312 | tf_op jit(solution)/shard_map/ppermute | solution.py:588
  526.0 18.8 %all-to-all-start.9 = ((bf16[16,8,2176]{2,1,0:T(8,128)(2,1)}), bf16[16,8,2176]{2,1,0:T(8,128)(2,1)S(1)}, u32[]{:S(2)}, u32[]{:S(2)}) async-start(bf16[16,8,2176]{2,1,0:T(8,128)(2,1)} %broadcast_in_dim.145), calls=%async_computation.10 | async-start | bytes 1114112 | tf_op jit(solution)/shard_map/all_to_all | solution.py:611
  544.8 17.3 %all-to-all-start.14 = ((bf16[16,8,4096]{2,1,0:T(8,128)(2,1)}), bf16[16,8,4096]{2,1,0:T(8,128)(2,1)}, u32[]{:S(2)}, u32[]{:S(2)}) async-start(bf16[16,8,4096]{2,1,0:T(8,128)(2,1)} %bitcast.684), calls=%async_computation.18 | async-start | bytes 2097152 | tf_op jit(solution)/shard_map/all_to_all | solution.py:605
  564.5 16.5 %all-to-all-start.15 = ((bf16[16,8,4096]{2,1,0:T(8,128)(2,1)}), bf16[16,8,4096]{2,1,0:T(8,128)(2,1)S(1)}, u32[]{:S(2)}, u32[]{:S(2)}) async-start(bf16[16,8,4096]{2,1,0:T(8,128)(2,1)} %broadcast_in_dim.148), calls=%async_computation.19 | async-start | bytes 2097152 | tf_op jit(solution)/shard_map/all_to_all | solution.py:611
  (183 other events, 1602.1 us)
Sparse Core Ops, SparseCore 0:
  16.3 38.4 all-gather.4
  57.1 32.0 all-gather.8
  91.6 32.1 all-gather.6
  125.9 49.6 all-gather.10
  234.5 38.0 reduce-scatter.8
  284.4 38.8 reduce-scatter.6
  363.6 38.0 reduce-scatter.4
  404.1 54.3 reduce-scatter.10
